TPU v7x, 32 devices: a whole 2x2x4 slice. The times are simulated.
32 devices in a mesh: dp: 8 (over z, x), fsdp: 4 (over y, core).
Axes of the slice: x: 2, y: 2, z: 4, core: 2. Of those that a mesh axis runs over, the one named last changes fastest.
Arguments:
- hidden_in: bfloat16 [65536, 256], P(('dp', 'fsdp')), may hold values from -6 to 6
- lengths: int32 [128, 6], P(('dp', 'fsdp')), may hold values from 1 to 256, 512 in all within a row
- grad_out: bfloat16 [65536, 256], P(('dp', 'fsdp')), may hold values from -6 to 6
- attn_weight: bfloat16 [2, 256, 768], P(None, ('dp', 'fsdp')), may hold values from -0.375 to 0.375
- attn_bias: bfloat16 [2, 2, 256], P(None, None, ('dp', 'fsdp')), may hold values from -2 to 2
- out_weight: bfloat16 [2, 256, 256], P(None, ('dp', 'fsdp')), may hold values from -1.5 to 1.5
- ffn_in: bfloat16 [2, 256, 1024], P(None, ('dp', 'fsdp')), may hold values from -0.375 to 0.375
- ffn_in_bias: bfloat16 [2, 1024], P(None, ('dp', 'fsdp')), may hold values from -2 to 2
- ffn_out: bfloat16 [2, 1024, 256], P(None, ('dp', 'fsdp')), may hold values from -0.1875 to 0.1875
- norm_gain: bfloat16 [2, 2, 256], P(None, None, ('dp', 'fsdp')), may hold values from 0.5 to 1.5
- shifts: bfloat16 [2, 4, 256], P(None, None, ('dp', 'fsdp')), may hold values from -2 to 2
Outputs:
- hidden_out: bfloat16 [65536, 256], P(('dp', 'fsdp'))
- grad_in: bfloat16 [65536, 256], P(('dp', 'fsdp'))
- attn_weight_grad: float32 [2, 256, 768], P(None, ('dp', 'fsdp'))
- attn_bias_grad: float32 [2, 2, 256], P(None, None, ('dp', 'fsdp'))
- out_weight_grad: float32 [2, 256, 256], P(None, ('dp', 'fsdp'))
- ffn_in_grad: float32 [2, 256, 1024], P(None, ('dp', 'fsdp'))
- ffn_in_bias_grad: float32 [2, 1024], P(None, ('dp', 'fsdp'))
- ffn_out_grad: float32 [2, 1024, 256], P(None, ('dp', 'fsdp'))
- norm_gain_grad: float32 [2, 2, 256], P(None, None, ('dp', 'fsdp'))
- shifts_grad: float32 [2, 4, 256], P(None, None, ('dp', 'fsdp'))
Inputs may be any that keep to these rules, and one draw needn't show every extreme that they name: `lengths`: every row's entries sum to 512 and its largest entry is 256; the last entry is the padding length.
All inputs are finite; a program needn't handle non-finite values.
Results may differ from a plain program's by a relative error of at most 0.014.
Values may be sent and summed in bfloat16 or wider, within the bound.
No kernel may reach another device: no remote copies, remote signals or barrier semaphores. Data moves between devices by JAX's collectives and lax.ppermute only.
A program may use at most 192 MiB of HBM per device.

v0:
```python
from functools import partial

import jax
import jax.numpy as jnp
from jax import lax
from jax.experimental import pallas as pl
from jax.experimental.pallas import tpu as pltpu
from jax.sharding import PartitionSpec as P

HEADS = 4
HD = 64
SEQ = 512
PAIR = 2 * HD
EXTRA = 16
HALF = SEQ // 2
HALVES = (slice(0, HALF), slice(HALF, SEQ))
FAR = -(2.0**100)
FLOOR = -1e20
EPSILON = 1e-12
PIECE = 256
SMALL = 128
GROUPS = (4, 8, 8)
DEVICES = 32
LOW = jnp.bfloat16
F32 = jnp.float32
MEMORY = 2**26


def dot_nn(left, right):
    return lax.dot_general(left, right, (((1,), (0,)), ((), ())), preferred_element_type=F32)


def dot_nt(left, right):
    return lax.dot_general(left, right, (((1,), (1,)), ((), ())), preferred_element_type=F32)


def dot_tn(left, right):
    return lax.dot_general(left, right, (((0,), (0,)), ((), ())), preferred_element_type=F32)


def pieces(total, size=PIECE):
    return [pl.ds(start, size) for start in range(0, total, size)]


def three_parts(values):
    first = values.astype(LOW).astype(F32)
    rest = values - first
    second = rest.astype(LOW).astype(F32)
    return first, second, rest - second


BELL = -0.5 / 0.6931471805599453


def gelu_parts(u):
    cumulative = 0.5 + 0.5 * lax.erf(u * 0.7071067811865476)
    slope = cumulative + (u * 0.3989422804014327) * jnp.exp2(u * u * BELL)
    return u * cumulative, slope


def inverse_of(values):
    guess = pl.reciprocal(values, approx=True)
    return guess * (2.0 - values * guess)


def longest_start(lengths_ref, row):
    begin, found = jnp.int32(0), jnp.int32(0)
    for entry in range(lengths_ref.shape[1]):
        size = lengths_ref[row, entry]
        found = jnp.where(size == HALF, begin, found)
        begin = begin + size
    return found


def segments(lengths_ref, row):
    places = lax.broadcasted_iota(jnp.int32, (1, SEQ), 1) + longest_start(lengths_ref, row)
    places = places & (SEQ - 1)
    bound = jnp.int32(0)
    segment = jnp.zeros((1, SEQ), jnp.int32)
    last = lengths_ref.shape[1] - 1
    for entry in range(last):
        bound = bound + lengths_ref[row, entry]
        segment = segment + (places >= bound).astype(jnp.int32)
    return segment, last


def head_rows(head):
    return slice(head * HD, (head + 1) * HD)


def attention_forward(row, lengths_ref, x, wt_ref, bias_ref, qa_ref, ka_ref, va_ref, ob_ref, lse_ref, s_ref, p_ref):
    width = HEADS * HD
    segment, last = segments(lengths_ref, row)
    pad = (segment == last).astype(F32)
    line = lax.broadcasted_iota(jnp.int32, (EXTRA, SEQ), 0)
    aug_q = jnp.where(line == segment, 1.0, 0.0).astype(LOW)
    seen = (line == segment) & (segment != last)
    aug_k = jnp.where(seen | (line > last), 0.0, FAR).astype(LOW)
    aug_v = jnp.where(line == 0, 1.0, 0.0).astype(LOW)
    rest = jnp.zeros((PAIR - HD - EXTRA, SEQ), LOW)
    for head in range(HEADS):
        qa_ref[head, HD : HD + EXTRA] = aug_q
        ka_ref[head, HD : HD + EXTRA] = aug_k
        va_ref[head, HD : HD + EXTRA] = aug_v
        qa_ref[head, HD + EXTRA : PAIR] = rest
        ka_ref[head, HD + EXTRA : PAIR] = rest
    for block, ref in enumerate((qa_ref, ka_ref, va_ref)):
        lines = slice(block * width, (block + 1) * width)
        bias = bias_ref[lines]
        value = dot_nt(wt_ref[lines], x) + jnp.concatenate([bias] * (SEQ // 128), 1)
        if block == 0:
            value = value * HD**-0.5
        value = value.astype(LOW)
        for head in range(HEADS):
            ref[head, 0:HD] = value[head_rows(head)]
        yield

    def scores(head):
        for half in HALVES:
            s_ref[head % 2, half] = dot_tn(ka_ref[head, :, half], qa_ref[head, :, half])

    def softmax(head):
        tops = []
        for half in HALVES:
            tops.append(jnp.maximum(jnp.max(s_ref[head % 2, half], 0, keepdims=True), FLOOR))
            p_ref[head % 2, half] = jnp.exp(s_ref[head % 2, half] - tops[-1]).astype(LOW)
        return tops

    scores(0)
    yield
    for head in range(HEADS):
        if head + 1 < HEADS:
            scores(head + 1)
            yield
        tops = softmax(head)
        yield
        for half, top in zip(HALVES, tops):
            out = dot_nn(va_ref[head, :, half], p_ref[head % 2, half])
            alone = pad[:, half]
            total = out[HD : HD + 1] + alone
            lse_ref[head : head + 1, half] = jnp.where(alone > 0, 0.0, top + jnp.log(total))
            own = alone * va_ref[head, 0:HD, half].astype(F32)
            ob_ref[head_rows(head), half] = (out[0:HD] * inverse_of(total) + own).astype(LOW)
        yield


def normal(values):
    centred = values - jnp.mean(values, -1, keepdims=True)
    inverse = lax.rsqrt(jnp.mean(centred * centred, -1, keepdims=True) + EPSILON)
    return centred * inverse, inverse


def normal_back(cotangent, unit, inverse, gains):
    scaled = cotangent * gains
    return inverse * (
        scaled
        - jnp.mean(scaled, -1, keepdims=True)
        - unit * jnp.mean(scaled * unit, -1, keepdims=True)
    )


def dense_forward(x_ref, ob_ref, wo_ref, wi_ref, wf_ref, small_ref, bi_ref, n1_ref, n2_ref, inv_ref, yb_ref, gb_ref, gp_ref, z_ref, work_ref, u_ref):
    small = lambda index: small_ref[pl.ds(index, 1)]
    work_ref[...] = dot_tn(ob_ref[...], wo_ref[...])
    yield
    for place in pieces(SEQ):
        unit, inverse = normal(x_ref[place].astype(F32) + work_ref[place] + small(4))
        n1_ref[place] = unit
        inv_ref[place, pl.ds(0, HD)] = jnp.broadcast_to(inverse, (PIECE, HD))
        y = unit * small(2) + small(5)
        yb_ref[place] = y.astype(LOW)
        work_ref[place] = y + small(6)
        yield
    columns = 256
    count = wi_ref.shape[1] // columns

    def into(step):
        u_ref[step % 2] = dot_nn(yb_ref[...], wi_ref[:, pl.ds(step * columns, columns)])

    into(0)
    yield
    for step in range(count):
        if step + 1 < count:
            into(step + 1)
            yield
        lanes = pl.ds(step * columns, columns)
        for place in pieces(SEQ, SMALL):
            g, slope = gelu_parts(u_ref[step % 2, place] + bi_ref[:, lanes])
            gb_ref[place, lanes] = g.astype(LOW)
            gp_ref[place, lanes] = slope.astype(LOW)
            yield
    work_ref[...] += dot_nn(gb_ref[...], wf_ref[...])
    yield
    for place in pieces(SEQ):
        unit, inverse = normal(work_ref[place])
        n2_ref[place] = unit
        inv_ref[place, pl.ds(HD, HD)] = jnp.broadcast_to(inverse, (PIECE, HD))
        z_ref[place] = (unit * small(3) + small(7)).astype(z_ref.dtype)
        yield


def fold(values):
    return jnp.sum(values.reshape(-1, 8, values.shape[-1]), 0)


def dense_backward(dz_ref, n1_ref, n2_ref, inv_ref, yb_ref, gb_ref, gp_ref, ob_ref, wo_ref, wi_ref, wf_ref, small_ref, dr_ref, dob_ref, gwo_ref, gwi_ref, gwf_ref, gsmall_ref, gbi_ref, low_ref, u_ref, du_ref, turned_ref):
    small = lambda index: small_ref[pl.ds(index, 1)]
    for place in pieces(SEQ):
        dz = dz_ref[place].astype(F32)
        unit = n2_ref[place]
        gsmall_ref[3] += fold(dz * unit)
        gsmall_ref[7] += fold(dz)
        dr = normal_back(dz, unit, inv_ref[place, pl.ds(HD, 1)], small(3))
        dr_ref[place] = dr
        df = dr.astype(LOW)
        low_ref[place] = df
        gsmall_ref[6] += fold(df.astype(F32))
        yield
    columns = 256
    count = wi_ref.shape[1] // columns

    def back(step):
        u_ref[step % 2] = dot_nt(low_ref[...], wf_ref[pl.ds(step * columns, columns)])

    back(0)
    turned_ref[0, 0 : low_ref.shape[1]] = low_ref[...].T
    width = low_ref.shape[1]
    turned_ref[1, 0:width] = yb_ref[...].T
    turned_ref[1, width:] = jnp.ones((EXTRA, SEQ), LOW)
    yield
    for step in range(count):
        if step + 1 < count:
            back(step + 1)
            yield
        lanes = pl.ds(step * columns, columns)
        gwf_ref[:, lanes] += dot_nn(turned_ref[0, 0:width], gb_ref[:, lanes])
        yield
        for place in pieces(SEQ, SMALL):
            du = (u_ref[step % 2, place] * gp_ref[place, lanes].astype(F32)).astype(LOW)
            du_ref[place, lanes] = du
        yield
        product = dot_nn(turned_ref[1], du_ref[:, lanes])
        gwi_ref[:, lanes] += product[0:width]
        gbi_ref[:, lanes] += product[width : width + 8]
        yield
    u_ref[0] = dot_nt(du_ref[...], wi_ref[...])
    yield
    for place in pieces(SEQ):
        dy = dr_ref[place] + u_ref[0, place]
        unit = n1_ref[place]
        gsmall_ref[2] += fold(dy * unit)
        gsmall_ref[5] += fold(dy)
        dr = normal_back(dy, unit, inv_ref[place, pl.ds(0, 1)], small(2))
        dr_ref[place] = dr
        da = dr.astype(LOW)
        low_ref[place] = da
        gsmall_ref[4] += fold(da.astype(F32))
        yield
    gwo_ref[...] += dot_nn(ob_ref[...], low_ref[...])
    dob_ref[...] = dot_nt(wo_ref[...], low_ref[...]).astype(LOW)
    yield


def attention_backward(row, lengths_ref, x, do_ref, ob_ref, qa_ref, ka_ref, va_ref, lse_ref, dqkv_ref, gwq_ref, gbias_ref, p_ref, ds_ref, s_ref):
    width = HEADS * HD
    segment, last = segments(lengths_ref, row)
    pad = (segment == last).astype(F32)

    def scores(head):
        for half in HALVES:
            s_ref[0, head % 2, half] = dot_tn(ka_ref[head, :, half], qa_ref[head, :, half])
            s_ref[1, head % 2, half] = dot_tn(
                va_ref[head, 0:HD, half], do_ref[head_rows(head), half]
            )

    def weigh(head):
        product = do_ref[head_rows(head)].astype(F32) * ob_ref[head_rows(head)].astype(F32)
        centre = jnp.sum(product, 0, keepdims=True)
        for half in HALVES:
            p = jnp.exp(s_ref[0, head % 2, half] - lse_ref[head : head + 1, half])
            p_ref[head % 2, half] = p.astype(LOW)
            ds_ref[head % 2, half] = (p * (s_ref[1, head % 2, half] - centre[:, half])).astype(LOW)

    scores(0)
    yield
    for head in range(HEADS):
        if head + 1 < HEADS:
            scores(head + 1)
            yield
        weigh(head)
        yield
        for half in HALVES:
            ds, do = ds_ref[head % 2, half], do_ref[head_rows(head), half]
            dq = dot_nn(ka_ref[head, 0:HD, half], ds) * HD**-0.5
            dk = dot_nt(qa_ref[head, 0:HD, half], ds)
            dv = dot_nt(do, p_ref[head % 2, half]) + pad[:, half] * do.astype(F32)
            for block, value in enumerate((dq, dk, dv)):
                at = block * width + head * HD
                dqkv_ref[at : at + HD, half] = value.astype(LOW)
        yield
    for index, block in enumerate((0, 2)):
        value = dqkv_ref[block * width : (block + 1) * width].astype(F32)
        parts = [value[:, at : at + 128] for at in range(0, SEQ, 128)]
        gbias_ref[index] += (parts[0] + parts[1]) + (parts[2] + parts[3])
    gwq_ref[...] += dot_nn(dqkv_ref[...], x)
    yield


def unpack_matrix(raw_ref, at, into_ref):
    width = into_ref.shape[0]
    for start in range(0, into_ref.shape[1], width):
        block = raw_ref[:, :, pl.ds(at + start, width)].astype(F32)
        block = block.reshape(GROUPS + (width,)).swapaxes(0, 1).reshape(width, width)
        into_ref[:, pl.ds(start, width)] = block.astype(LOW)


def unpack_stacked(raw_ref, at, into_ref):
    width = into_ref.shape[1]
    count = into_ref.shape[0] // width
    blocks = [
        raw_ref[:, :, pl.ds(at + step * width, width)].astype(F32).reshape(GROUPS + (width,))
        for step in range(count)
    ]
    outer, inner, rows = GROUPS
    for place in range(inner):
        part = jnp.stack([jnp.stack([block[f, place] for block in blocks]) for f in range(outer)])
        size = outer * count * rows
        into_ref[pl.ds(place * size, size)] = part.reshape(size, width).astype(LOW)


def counter(shape, axis):
    return lax.broadcasted_iota(jnp.int32, shape, axis)


def split_by(values, size):
    return lax.shift_right_logical(values, size.bit_length() - 1), values & (size - 1)


def sources(rows):
    outer, inner, height = GROUPS
    group, within = split_by(counter((rows, 1), 0), height)
    far, near = split_by(group, inner)
    return near * outer + far, within


def unpack_vectors(raw_ref, at, layer):
    outer, inner, rows = GROUPS
    total = outer * inner * rows
    raw = raw_ref[:, :, pl.ds(at, 128)].reshape(total, 128)
    owner, place = split_by(counter((1, total), 1), rows)
    pick = jnp.where(counter((128, 1), 0) == rows * layer + place, 1.0, 0.0).astype(LOW)
    device, unused = sources(total)
    spread = jnp.where(owner == device, dot_nn(raw, pick), 0.0)
    return jnp.sum(spread.reshape(outer * inner, rows, total), 0)


def unpack_hidden(raw_ref, at, layer, hidden):
    outer, inner, rows = GROUPS
    total = outer * inner * rows
    raw = raw_ref[:, :, pl.ds(at, 128)].reshape(total, 128)
    owner, place = split_by(counter((1, hidden), 1), hidden // (outer * inner))
    pick = jnp.where(counter((128, 1), 0) == 2 * rows + place, 1.0, 0.0).astype(LOW)
    device, within = sources(total)
    device = jnp.where(within == layer, device, -1)
    spread = jnp.where(owner == device, dot_nn(raw, pick), 0.0)
    return jnp.sum(spread, 0, keepdims=True)


def pack_matrix(sum_ref, sent_ref, at, turned=False):
    width = sum_ref.shape[1 if turned else 0]
    outer, inner, rows = GROUPS
    for start in range(0, sum_ref.shape[0 if turned else 1], width):
        near = pl.ds(start, width)
        block = sum_ref[near].T if turned else sum_ref[:, near]
        block = block.reshape(inner, outer, rows, width)
        block = block.swapaxes(0, 1).reshape(outer, inner * rows, width)
        sent_ref[:, :, pl.ds(at + start, width)] = block.astype(LOW)


def pack_stacked(sum_ref, sent_ref, at):
    width = sum_ref.shape[0]
    outer, inner, rows = GROUPS
    count = sum_ref.shape[1] // width
    near = inner // count
    for step in range(count):
        block = sum_ref[:, pl.ds(step * width, width)].T
        block = block.reshape(near, outer, count, rows, width)
        for part in range(count):
            piece = jnp.stack([block[:, f, part] for f in range(outer)])
            piece = piece.reshape(outer, near * rows, width)
            sent_ref[:, pl.ds(step * near * rows, near * rows), pl.ds(at + part * width, width)] = (
                piece.astype(LOW)
            )


def pack_vectors(block, line, sent_ref, at):
    outer, inner, rows = GROUPS
    total = outer * inner * rows
    device, within = sources(total)
    owner, unused = split_by(counter((1, total), 1), rows)
    spread = jnp.broadcast_to(block[None], (outer * inner, rows, total)).reshape(total, total)
    spread = jnp.where(owner == device, spread, 0.0).astype(LOW)
    unused, place = split_by(counter((total, 1), 0), rows)
    found = dot_nn(spread, jnp.where(counter((1, 128), 1) == place, 1.0, 0.0).astype(LOW))
    if line is not None:
        hidden = line.shape[1]
        height = hidden // (outer * inner)
        owner, unused = split_by(counter((1, hidden), 1), height)
        spread = jnp.where(owner == jnp.where(within == 0, device, -1), line, 0.0).astype(LOW)
        unused, place = split_by(counter((hidden, 1), 0), height)
        pick = jnp.where(counter((1, 128), 1) == 2 * rows + place, 1.0, 0.0).astype(LOW)
        found = found + dot_nn(spread, pick)
    sent_ref[:, :, pl.ds(at, 128)] = found.reshape(outer, inner * rows, 128).astype(LOW)


def bias_rows(gbias_ref):
    width = gbias_ref.shape[1]
    parts = [jnp.sum(gbias_ref[index].T, 0, keepdims=True) for index in range(2)]
    return jnp.concatenate(parts + [jnp.zeros((6, width), F32)], 0)


def pack_dense(gwo_ref, gwi_ref, gwf_ref, gsmall_ref, gbi_ref, block, sent_ref, at):
    width, hidden = gwi_ref.shape
    pack_matrix(gwo_ref, sent_ref, at)
    pack_matrix(gwi_ref, sent_ref, at + width)
    pack_stacked(gwf_ref, sent_ref, at + width + hidden)
    block = jnp.sum(gsmall_ref[...], 1) + block
    pack_vectors(block, gbi_ref[0:1], sent_ref, at + width + 2 * hidden)


def shape_of(array):
    return jax.ShapeDtypeStruct(array.shape, array.dtype)


def by_row(shape, group):
    if len(shape) == 2:
        return pl.BlockSpec((group * SEQ, shape[1]), lambda step: (step, 0))
    return pl.BlockSpec((group,) + tuple(shape[1:]), lambda step: (step,) + (0,) * (len(shape) - 1))


def one_row(ref, member):
    if len(ref.shape) == 2:
        return ref.at[pl.ds(member * SEQ, SEQ)]
    return ref.at[member]


def alternate(runs):
    running = []
    waiting = list(runs)
    while running or waiting:
        if waiting:
            running.append(waiting.pop(0))
        for run in list(running):
            try:
                next(run)
            except StopIteration:
                running.remove(run)


def whole(shape):
    return pl.BlockSpec(tuple(shape), lambda row: (0,) * len(shape))


def run_rows(
    body, lengths, rowwise, fixed, row_outs, sent, shared, private, cost, setup, finish, after=(),
    scalars=(), group=1
):
    count = lengths.shape[0]
    group = group if count % group == 0 else 1
    cuts = [len(scalars), len(rowwise), len(fixed), len(after), len(row_outs), len(sent)]
    cuts += [len(shared)] + [len(private)] * group

    def kernel(lengths_ref, *refs):
        step = pl.program_id(0)
        groups = []
        at = 0
        for cut in cuts:
            groups.append(refs[at : at + cut])
            at += cut
        numbers, rows_in, fixed_in, unused, rows_out, sent_out, work = groups[:7]

        @pl.when(step == 0)
        def _():
            setup(numbers, fixed_in, sent_out, work)

        alternate(
            body(
                step * group + member,
                lengths_ref,
                [one_row(ref, member) for ref in rows_in],
                [one_row(ref, member) for ref in rows_out],
                work,
                groups[7 + member],
            )
            for member in range(group)
        )

        if finish:

            @pl.when(step == count // group - 1)
            def _():
                finish(numbers, work, sent_out)

    return pl.pallas_call(
        kernel,
        grid=(count // group,),
        in_specs=[pl.BlockSpec(memory_space=pltpu.SMEM)] * (1 + len(scalars))
        + [by_row(array.shape, group) for array in rowwise]
        + [whole(array.shape) for array in fixed]
        + [pl.BlockSpec(memory_space=pl.ANY) for array in after],
        out_specs=[by_row(part.shape, group) for part in row_outs]
        + [whole(part.shape) for part in sent],
        out_shape=list(row_outs) + list(sent),
        scratch_shapes=list(shared) + list(private) * group,
        compiler_params=pltpu.CompilerParams(
            dimension_semantics=("arbitrary",), vmem_limit_bytes=MEMORY
        ),
        cost_estimate=pl.CostEstimate(flops=cost, bytes_accessed=8 * 2**20, transcendentals=0),
    )(lengths, *scalars, *rowwise, *fixed, *after)


def struct(shape, dtype):
    return jax.ShapeDtypeStruct(tuple(shape), dtype)


FORWARD_SCRATCH = lambda: [
    pltpu.VMEM((2, SEQ, HALF), F32),
    pltpu.VMEM((2, SEQ, HALF), LOW),
]
BACKWARD_SCRATCH = lambda: [
    pltpu.VMEM((2, SEQ, HALF), LOW),
    pltpu.VMEM((2, SEQ, HALF), LOW),
    pltpu.VMEM((2, 2, SEQ, HALF), F32),
    pltpu.VMEM((3 * HEADS * HD, SEQ), LOW),
]


def attention_outs(rows, width):
    return [
        struct((rows, HEADS, PAIR, SEQ), LOW),
        struct((rows, HEADS, PAIR, SEQ), LOW),
        struct((rows, HEADS, HD + EXTRA, SEQ), LOW),
        struct((rows, width, SEQ), LOW),
        struct((rows, 8, SEQ), F32),
    ]


def dense_outs(tokens, width, hidden):
    return [
        struct((tokens, width), F32),
        struct((tokens, width), F32),
        struct((tokens, PAIR), F32),
        struct((tokens, width), LOW),
        struct((tokens, hidden), LOW),
        struct((tokens, hidden), LOW),
    ]


def vmem(shape, dtype):
    return pltpu.VMEM(tuple(shape), dtype)


def attention_weights(width):
    return [vmem((width, 3 * width), LOW), vmem((3 * width, width), LOW), vmem((3 * width, 128), F32)]


def dense_weights(width, hidden):
    return [
        vmem((width, width), LOW),
        vmem((width, hidden), LOW),
        vmem((hidden, width), LOW),
        vmem((8, width), F32),
        vmem((1, hidden), F32),
    ]


def dense_sums(width, hidden):
    return [
        vmem((width, width), F32),
        vmem((width, hidden), F32),
        vmem((width, hidden), F32),
        vmem((8, 8, width), F32),
        vmem((8, hidden), F32),
    ]


def attention_sums(width):
    return [vmem((3 * width, width), F32), vmem((2, width, 128), F32)]


def dense_work(width, hidden):
    return [
        vmem((SEQ, width), LOW),
        vmem((2, SEQ, width), F32),
        vmem((SEQ, hidden), LOW),
        vmem((2, width + EXTRA, SEQ), LOW),
    ]


def set_attention(layer, urgent_ref, raw_ref, at, wq_ref, wt_ref, bias_ref):
    width = wq_ref.shape[0]
    unpack_matrix(raw_ref, at, wq_ref)
    vectors = unpack_vectors(urgent_ref, 3 * width, layer)
    for block, line in enumerate((vectors[0:1], jnp.zeros((1, width), F32), vectors[1:2])):
        lines = pl.ds(block * width, width)
        wt_ref[lines] = wq_ref[:, lines].astype(F32).T.astype(LOW)
        bias_ref[lines] = jnp.broadcast_to(line, (128, width)).T


def set_dense(layer, urgent_ref, raw_ref, at, wo_ref, wi_ref, wf_ref, small_ref, bi_ref):
    width, hidden = wi_ref.shape
    unpack_matrix(raw_ref, at, wo_ref)
    unpack_matrix(raw_ref, at + width, wi_ref)
    unpack_stacked(raw_ref, at + width + hidden, wf_ref)
    small_ref[...] = unpack_vectors(urgent_ref, 3 * width, layer)
    bi_ref[...] = unpack_hidden(urgent_ref, 3 * width, layer, hidden)


def clear(refs):
    for ref in refs:
        ref[...] = jnp.zeros(ref.shape, ref.dtype)


def assemble(place_ref, part_refs, into_ref):
    for step, ref in enumerate(part_refs):
        into_ref[place_ref[0] ^ step] = ref[...]


def raw_block(parts):
    return vmem((len(parts),) + parts[0].shape, LOW)


def turned_back(lengths_ref, row, values):
    return pltpu.roll(values, longest_start(lengths_ref, row), 0).astype(LOW)


def rotate_kernel(lengths, arrays):
    def body(row, lengths_ref, rowwise, outs, work, own):
        back = (SEQ - longest_start(lengths_ref, row)) & (SEQ - 1)
        for source, target in zip(rowwise, outs):
            target[...] = pltpu.roll(source[...].astype(F32), back, 0).astype(LOW)
            yield

    return run_rows(
        body, lengths, list(arrays), [], [struct(array.shape, LOW) for array in arrays], [], [], [],
        10**6, lambda *refs: None, None,
    )


def first_kernel(lengths, x, place, parts):
    rows, (tokens, width) = lengths.shape[0], x.shape

    def setup(numbers, fixed, sent, work):
        assemble(numbers[0], fixed, sent[0])
        set_attention(0, sent[0], sent[0], 0, *work)

    def body(row, lengths_ref, rowwise, outs, work, own):
        return attention_forward(row, lengths_ref, rowwise[0][...], *work[1:3], *outs, *own)

    return run_rows(
        body, lengths, [x], list(parts), attention_outs(rows, width),
        [struct((len(parts),) + parts[0].shape, LOW)],
        attention_weights(width), FORWARD_SCRATCH(), 4 * 10**9, setup, None, (), [place],
    )


def attention_kernel(layer, lengths, x, place, urgent, parts, at):
    rows, (tokens, width) = lengths.shape[0], x.shape

    def setup(numbers, fixed, sent, work):
        assemble(numbers[0], fixed[1:], work[3])
        set_attention(layer, fixed[0], work[3], at, *work[:3])

    def body(row, lengths_ref, rowwise, outs, work, own):
        return attention_forward(
            row, lengths_ref, rowwise[0][...].astype(LOW), *work[1:3], *outs, *own
        )

    return run_rows(
        body, lengths, [x], [urgent] + list(parts), attention_outs(rows, width), [],
        attention_weights(width) + [raw_block(parts)], FORWARD_SCRATCH(),
        4 * 10**9, setup, None, (), [place],
    )


def dense_kernel(layer, lengths, x, ob, place, urgent, parts, at, hidden):
    tokens, width = x.shape

    def setup(numbers, fixed, sent, work):
        assemble(numbers[0], fixed[1:], work[5])
        set_dense(layer, fixed[0], work[5], at, *work[:5])

    def body(row, lengths_ref, rowwise, outs, work, own):
        return dense_forward(*rowwise, *work[:5], *outs, *own)

    return run_rows(
        body, lengths, [x, ob], [urgent] + list(parts),
        dense_outs(tokens, width, hidden) + [struct((tokens, width), F32)], [],
        dense_weights(width, hidden) + [raw_block(parts)],
        [vmem((SEQ, width), F32), vmem((2, SEQ, width), F32)],
        5 * 10**9, setup, None, (), [place],
    )


def turn_kernel(layer, lengths, x, ob, cotangent, place, urgent, parts, at, hidden):
    tokens, width = x.shape
    columns = width + 2 * hidden + 128

    def setup(numbers, fixed, sent, work):
        assemble(numbers[0], fixed[1:], work[11])
        set_dense(layer, fixed[0], work[11], at, *work[:5])
        clear(work[5:10])

    def body(row, lengths_ref, rowwise, outs, work, own):
        x_ref, ob_ref, dz_ref = rowwise
        z_ref, dr_ref, dob_ref = outs
        weights, sums = work[:5], work[5:10]
        kept, work_ref, back = own[:6], own[6], own[7:]
        yield from dense_forward(x_ref, ob_ref, *weights, *kept, z_ref, work_ref, back[1])
        yield from dense_backward(dz_ref, *kept, ob_ref, *weights[:4], dr_ref, dob_ref, *sums, *back)

    def finish(numbers, work, sent):
        pack_dense(*work[5:10], 0.0, work[10], 0)
        hand_out(numbers[0], work[10], sent)

    kept = [vmem((SEQ,) + part.shape[1:], part.dtype) for part in dense_outs(tokens, width, hidden)]
    return run_rows(
        body, lengths, [x, ob, cotangent], [urgent] + list(parts),
        [struct((tokens, width), LOW), struct((tokens, width), F32), struct((tokens // SEQ, width, SEQ), LOW)],
        [struct((64, columns), LOW)] * 4,
        dense_weights(width, hidden) + dense_sums(width, hidden)
        + [vmem((4, 64, columns), LOW), raw_block(parts)],
        kept + [vmem((SEQ, width), F32)] + dense_work(width, hidden),
        10**10, setup, finish, (), [place], 2,
    )


def hand_out(place_ref, packed_ref, sent):
    for step, ref in enumerate(sent):
        ref[...] = packed_ref[place_ref[0] ^ step]


def middle_kernel(lengths, upper, lower, place, urgent, parts, hidden, after):
    tokens, width = upper[0].shape
    columns = 4 * width + 2 * hidden + 128

    def setup(numbers, fixed, sent, work):
        assemble(numbers[0], fixed[1:], work[16])
        set_attention(1, fixed[0], work[16], 0, *work[:3])
        set_dense(0, fixed[0], work[16], 3 * width, *work[3:8])
        clear(work[8:15])

    def body(row, lengths_ref, rowwise, outs, work, own):
        up, low = rowwise[:8], rowwise[8:]
        dx_ref = own[0]
        yield from attention_backward(
            row, lengths_ref, up[0][...].astype(LOW), *up[1:7], own[-1], *work[8:10], *own[5:-1]
        )
        dx_ref[...] = up[7][...] + dot_tn(own[-1][...], work[1][...])
        yield
        yield from dense_backward(dx_ref, *low, *work[3:7], *outs, *work[10:15], *own[1:5])

    def finish(numbers, work, sent):
        pack_matrix(work[8], work[15], 0, True)
        pack_dense(*work[10:15], bias_rows(work[9]), work[15], 3 * width)
        hand_out(numbers[0], work[15], sent)

    return run_rows(
        body, lengths, list(upper) + list(lower), [urgent] + list(parts),
        [struct((tokens, width), F32), struct((tokens // SEQ, width, SEQ), LOW)],
        [struct((64, columns), LOW)] * 4,
        attention_weights(width) + dense_weights(width, hidden)
        + attention_sums(width) + dense_sums(width, hidden)
        + [vmem((4, 64, columns), LOW), raw_block(parts)],
        [vmem((SEQ, width), F32)] + dense_work(width, hidden) + BACKWARD_SCRATCH(),
        15 * 10**9, setup, finish, after, [place], 2,
    )


def last_kernel(lengths, upper, after, place):
    tokens, width = upper[0].shape

    def setup(numbers, fixed, sent, work):
        clear(work[:2])

    def body(row, lengths_ref, rowwise, outs, work, own):
        return attention_backward(
            row, lengths_ref, rowwise[0][...], *rowwise[1:], outs[0], *work[:2], *own
        )

    def finish(numbers, work, sent):
        pack_matrix(work[0], work[2], 0, True)
        pack_vectors(bias_rows(work[1]), None, work[2], 3 * width)
        hand_out(numbers[0], work[2], sent)

    return run_rows(
        body, lengths, list(upper), [], [struct((tokens // SEQ, 3 * width, SEQ), LOW)],
        [struct((64, 3 * width + 128), LOW)] * 4,
        attention_sums(width) + [vmem((4, 64, 3 * width + 128), LOW)],
        BACKWARD_SCRATCH()[:-1], 8 * 10**9, setup, finish, after, [place], 2,
    )


def outward_kernel(lengths, z, after):
    def body(row, lengths_ref, rowwise, outs, work, own):
        outs[0][...] = turned_back(lengths_ref, row, rowwise[0][...].astype(F32))
        yield

    (found,) = run_rows(
        body, lengths, [z], [], [struct(z.shape, LOW)], [], [], [], 3 * 10**9,
        lambda *refs: None, None, after,
    )
    return found


def inward_kernel(lengths, dqkv, dr, urgent, after):
    tokens, width = dr.shape

    def setup(numbers, fixed, sent, work):
        set_attention(0, fixed[0], fixed[0], 0, *work)

    def body(row, lengths_ref, rowwise, outs, work, own):
        dqkv_ref, dr_ref = rowwise
        dx = dr_ref[...] + dot_tn(dqkv_ref[...], work[1][...])
        outs[0][...] = turned_back(lengths_ref, row, dx)
        yield

    (found,) = run_rows(
        body, lengths, [dqkv, dr], [urgent], [struct((tokens, width), LOW)], [],
        attention_weights(width), [], 10**10, setup, None, after,
    )
    return found


def hold(array, after):
    def kernel(*refs):
        pass

    anywhere = pl.BlockSpec(memory_space=pl.ANY)
    return pl.pallas_call(
        kernel,
        in_specs=[anywhere] * (1 + len(after)),
        out_specs=anywhere,
        out_shape=shape_of(array),
        input_output_aliases={0: 0},
    )(array, *after)


def pack_parameters(
    attn_weight, attn_bias, out_weight, ffn_in, ffn_in_bias, ffn_out, norm_gain, shifts
):
    depth, rows, width = out_weight.shape
    copies = GROUPS[1]
    hidden = ffn_in.shape[2]
    dense = width + 2 * hidden
    height = ffn_in_bias.shape[1]

    def kernel(wq_ref, ab_ref, wo_ref, wi_ref, bi_ref, wf_ref, gain_ref, shift_ref, first_ref, rest_ref, small_ref):
        def put(ref, block, at):
            block = jnp.broadcast_to(block.astype(F32)[None], (copies,) + block.shape)
            block = block.reshape(copies * block.shape[1], block.shape[2])
            ref[:, pl.ds(at, block.shape[1])] = block.astype(LOW)

        small_ref[...] = jnp.zeros(small_ref.shape, F32)
        for layer in range(depth):
            lanes = pl.ds(rows * layer, rows)
            small_ref[0:2, lanes] = ab_ref[layer].astype(F32)
            small_ref[2:4, lanes] = gain_ref[layer].astype(F32)
            small_ref[4:8, lanes] = shift_ref[layer].astype(F32)
        small_ref[0:depth, pl.ds(2 * rows, height)] = bi_ref[...].astype(F32)
        put(first_ref, wq_ref[0], 0)
        put(first_ref, small_ref[...], 3 * width)
        put(first_ref, wq_ref[1], 3 * width + 128)
        for layer, ref, at in ((0, first_ref, 6 * width + 128), (1, rest_ref, 0)):
            put(ref, wo_ref[layer], at)
            put(ref, wi_ref[layer], at + width)
            at += width + hidden
            down = wf_ref[layer].astype(F32)
            for step in range(hidden // width):
                put(ref, down[step * rows : (step + 1) * rows], at)
                at += width

    return pl.pallas_call(
        kernel,
        in_specs=[pl.BlockSpec(memory_space=pltpu.VMEM)] * 8,
        out_shape=[
            struct((copies * rows, 6 * width + 128 + dense), LOW),
            struct((copies * rows, dense), LOW),
        ],
        scratch_shapes=[vmem((rows, 128), F32)],
        compiler_params=pltpu.CompilerParams(vmem_limit_bytes=MEMORY),
    )(attn_weight, attn_bias, out_weight, ffn_in, ffn_in_bias, ffn_out, norm_gain, shifts)


def add_parts(place, parts, halves, after=()):
    lanes = parts[0].shape[1]
    count = len(parts)
    many, rows = GROUPS[1:]
    outs = 2 if halves else 1

    def kernel(place_ref, *refs):
        out_refs, sum_ref = refs[count + len(after) : -1], refs[-1]
        bit = place_ref[0] & 1
        for start in range(0, lanes, 128):
            near = pl.ds(start, 128)
            total = refs[0][:, near].astype(F32)
            for ref in refs[1:count]:
                total = total + ref[:, near].astype(F32)
            if halves:
                sum_ref[:, :, near] = total.reshape(many, rows, 128)
            else:
                out_refs[0][:, near] = total.astype(LOW)
        for side, ref in enumerate(out_refs if halves else ()):
            for start in range(0, lanes, 128):
                near = pl.ds(start, 128)
                block = [sum_ref[2 * step + (bit ^ side), :, near] for step in range(many // 2)]
                ref[:, near] = jnp.concatenate(block, 0).astype(LOW)

    return pl.pallas_call(
        kernel,
        in_specs=[pl.BlockSpec(memory_space=pltpu.SMEM)]
        + [pl.BlockSpec(memory_space=pltpu.VMEM)] * count
        + [pl.BlockSpec(memory_space=pl.ANY)] * len(after),
        out_shape=[struct((many * rows // outs, lanes), LOW)] * outs,
        scratch_shapes=[vmem((many, rows, lanes), F32)],
        compiler_params=pltpu.CompilerParams(vmem_limit_bytes=MEMORY),
    )(place, *parts, *after)


def add_halves(place, pairs, after=()):
    many, rows = GROUPS[1] // 2, GROUPS[2]
    widths = [pair[0].shape[1] for pair in pairs]
    lanes = sum(widths)

    def kernel(place_ref, *refs):
        out_refs, sum_ref = refs[2 * len(pairs) + len(after) : -1], refs[-1]
        at = 0
        for index, size in enumerate(widths):
            for start in range(0, size, 128):
                near = pl.ds(start, 128)
                total = refs[2 * index][:, near].astype(F32) + refs[2 * index + 1][:, near].astype(F32)
                sum_ref[:, :, pl.ds(at + start, 128)] = total.reshape(many, rows, 128)
            at += size
        far = lax.shift_right_logical(place_ref[0], 1)
        for step, ref in enumerate(out_refs):
            ref[...] = sum_ref[far ^ step].astype(LOW)

    return pl.pallas_call(
        kernel,
        in_specs=[pl.BlockSpec(memory_space=pltpu.SMEM)]
        + [pl.BlockSpec(memory_space=pltpu.VMEM)] * (2 * len(pairs))
        + [pl.BlockSpec(memory_space=pl.ANY)] * len(after),
        out_shape=[struct((rows, lanes), LOW)] * many,
        scratch_shapes=[vmem((many, rows, lanes), F32)],
        compiler_params=pltpu.CompilerParams(vmem_limit_bytes=MEMORY),
    )(place, *(part for pair in pairs for part in pair), *after)


def write_gradients(found, depth, width, hidden, after):
    rows = GROUPS[2]
    height = hidden // DEVICES
    dense = width + 2 * hidden

    def kernel(*refs):
        found_refs, refs = refs[: len(found)], refs[len(found) + len(after) :]
        gwq_ref, gab_ref, gwo_ref, gwi_ref, gbi_ref, gwf_ref, gain_ref, shift_ref = refs

        def total(at, columns):
            value = found_refs[0][:, pl.ds(at, columns)].astype(F32)
            for ref in found_refs[1:]:
                value = value + ref[:, pl.ds(at, columns)].astype(F32)
            return value

        first, second = dense + 128, 2 * dense + 3 * width + 256
        blocks = [total(at, 128) for at in (dense, first + 3 * width + dense, second + 3 * width)]
        for layer, at, block in ((0, second, blocks[2]), (1, first, blocks[1])):
            gwq_ref[layer] = total(at, 3 * width)
            gab_ref[layer] = block[0:2, 0:rows]
        for layer, at, block in ((0, first + 3 * width, blocks[1]), (1, 0, blocks[0])):
            gwo_ref[layer] = total(at, width)
            gwi_ref[layer] = total(at + width, hidden)
            for step in range(hidden // width):
                gwf_ref[layer, pl.ds(step * rows, rows)] = total(
                    at + width + hidden + step * width, width
                )
            gain_ref[layer] = block[2:4, 0:rows]
            shift_ref[layer] = block[4:8, 0:rows]
            gbi_ref[pl.ds(layer, 1)] = pltpu.roll(block, 128 - 2 * rows, 1)[0:1, 0:height]

    outs = [
        struct((depth, rows, 3 * width), F32),
        struct((depth, 2, rows), F32),
        struct((depth, rows, width), F32),
        struct((depth, rows, hidden), F32),
        struct((depth, height), F32),
        struct((depth, height, width), F32),
        struct((depth, 2, rows), F32),
        struct((depth, 4, rows), F32),
    ]
    return pl.pallas_call(
        kernel,
        in_specs=[pl.BlockSpec(memory_space=pltpu.VMEM)] * len(found)
        + [pl.BlockSpec(memory_space=pl.ANY)] * len(after),
        out_shape=outs,
        compiler_params=pltpu.CompilerParams(vmem_limit_bytes=MEMORY),
    )(*found, *after)


def exchange(parts, axis):
    return lax.all_to_all(parts, axis, 0, 0, tiled=True)


def swap(part, axis, step):
    size = lax.axis_size(axis)
    return lax.ppermute(part, axis, [(source, source ^ step) for source in range(size)])


def local(
    hidden_in,
    lengths,
    grad_out,
    attn_weight,
    attn_bias,
    out_weight,
    ffn_in,
    ffn_in_bias,
    ffn_out,
    norm_gain,
    shifts,
):
    depth, rows, width = out_weight.shape
    hidden = ffn_in.shape[2]
    first, second = lax.axis_size("dp"), lax.axis_size("fsdp")
    fits = (second, first, rows) == GROUPS
    urgent_size = 3 * width + 128
    if fits:
        early, later = pack_parameters(
            attn_weight, attn_bias, out_weight, ffn_in, ffn_in_bias, ffn_out, norm_gain, shifts
        )
        across = lax.axis_index("dp").astype(jnp.int32).reshape(1)
        place = lax.axis_index("fsdp").astype(jnp.int32).reshape(1)
        partners = range(1, second)
        x0, dz1 = rotate_kernel(lengths, (hidden_in, grad_out))
        early = hold(exchange(early, "dp"), (x0,))
        urgent = early[:, :urgent_size]
        urgent = [urgent] + [swap(urgent, "fsdp", step) for step in partners]
        raw0 = early[:, urgent_size:]
        raw0 = [raw0, swap(raw0, "fsdp", 1), swap(raw0, "fsdp", 2)]
    else:
        urgent, raw0, raw1 = gather_other(
            attn_weight, attn_bias, out_weight, ffn_in, ffn_in_bias, ffn_out, norm_gain, shifts
        )
        urgent, raw0, raw1 = ([part[step] for step in range(4)] for part in (urgent, raw0, raw1))
        place = jnp.zeros((1,), jnp.int32)
        x0, dz1 = rotate_kernel(lengths, (hidden_in, grad_out))

    qa0, ka0, va0, ob0, lse0, urgent = first_kernel(lengths, x0, place, urgent)
    if fits:
        raw0[2] = hold(raw0[2], (ob0,))
        raw0.append(swap(raw0[2], "fsdp", 1))
        later = exchange(hold(later, (ob0,)), "dp")
    n1, n2, inv, yb, gb, gp, z0 = dense_kernel(
        0, lengths, x0, ob0, place, urgent, raw0, 3 * width, hidden
    )
    if fits:
        raw1 = hold(later, (z0,))
        raw1 = [raw1, swap(raw1, "fsdp", 1), swap(raw1, "fsdp", 2)]
    qa1, ka1, va1, ob1, lse1 = attention_kernel(1, lengths, z0, place, urgent, raw0, 0)
    if fits:
        raw1[2] = hold(raw1[2], (ob1,))
        raw1.append(swap(raw1[2], "fsdp", 1))
    z1, dr1, dob1, *sent_a = turn_kernel(
        1, lengths, z0, ob1, dz1, place, urgent, raw1, 0, hidden
    )
    dr0, dob0, *sent_b = middle_kernel(
        lengths,
        (z0, dob1, ob1, qa1, ka1, va1, lse1, dr1),
        (n1, n2, inv, yb, gb, gp, ob0),
        place,
        urgent,
        raw0,
        hidden,
        (sent_a[0],),
    )
    if fits:
        got_a = [sent_a[0]] + [swap(sent_a[step], "fsdp", step) for step in partners]
        keep_a, give_a = add_parts(across, got_a, True, (sent_b[0],))
        got_ax = swap(give_a, "dp", 1)
        ready = (sent_b[0], keep_a)
    else:
        ready = ()
    dqkv, *sent_c = last_kernel(
        lengths, (x0, dob0, ob0, qa0, ka0, va0, lse0), ready, place
    )
    if fits:
        got_b = [sent_b[0]] + [swap(sent_b[step], "fsdp", step) for step in partners]
        got_c = [sent_c[0]] + [swap(sent_c[step], "fsdp", step) for step in partners]
        keep_b, give_b = add_parts(across, got_b, True, (got_ax, dqkv))
        keep_c, give_c = add_parts(across, got_c, True, (keep_b,))
        grad_in = inward_kernel(lengths, dqkv, dr0, urgent, (keep_c,))
        pairs = [(keep_a, got_ax), (keep_b, swap(give_b, "dp", 1)), (keep_c, swap(give_c, "dp", 1))]
        found = add_halves(across, pairs, (grad_in,))
        hidden_out = outward_kernel(lengths, z1, (found[0],))
        found = [found[0]] + [swap(found[step], "dp", 2 * step) for step in range(1, first // 2)]
        grads = write_gradients(found, depth, width, hidden, (hidden_out,))
    else:
        grad_in = inward_kernel(lengths, dqkv, dr0, urgent, ())
        hidden_out = outward_kernel(lengths, z1, ())
        grads = scatter_other(
            *(jnp.stack(part) for part in (sent_a, sent_b, sent_c)), rows, width, hidden
        )
    return (hidden_out, grad_in, *grads)


def gather_other(
    attn_weight, attn_bias, out_weight, ffn_in, ffn_in_bias, ffn_out, norm_gain, shifts
):
    axes = ("dp", "fsdp")
    gather = lambda part, axis: lax.all_gather(part, axes, axis=axis, tiled=True)
    depth, unused, width = out_weight.shape
    hidden = ffn_in.shape[2]
    outer, inner, rows = GROUPS
    vectors = gather(jnp.concatenate([attn_bias, norm_gain, shifts], 1), 2)
    line = gather(ffn_in_bias, 1)

    def order(natural):
        return (
            natural.reshape(inner, outer, rows, -1).swapaxes(0, 1).reshape(outer, inner * rows, -1)
        )

    def stacked(part):
        part = part.reshape(DEVICES, -1, rows, width)
        return order(part.swapaxes(1, 2).reshape(width, -1))

    small = vectors.reshape(depth, 8, DEVICES, rows).transpose(2, 1, 0, 3).reshape(width, -1)
    line = line.reshape(depth, DEVICES, -1).swapaxes(0, 1)
    line = jnp.pad(line, ((0, 0), (0, 8 - depth), (0, 0))).reshape(width, -1)
    small = jnp.concatenate([small, line], 1)
    small = jnp.pad(small, ((0, 0), (0, 128 - small.shape[1])))
    wq, wo, wi, wf = (gather(part, 1) for part in (attn_weight, out_weight, ffn_in, ffn_out))
    urgent = jnp.concatenate([order(wq[0]), order(small)], 2)
    raw0 = jnp.concatenate([order(wq[1]), order(wo[0]), order(wi[0]), stacked(wf[0])], 2)
    raw1 = jnp.concatenate([order(wo[1]), order(wi[1]), stacked(wf[1])], 2)
    return urgent, raw0, raw1


def scatter_other(sent_a, sent_b, sent_c, own_rows, width, hidden):
    outer, inner, rows = GROUPS
    axes = ("dp", "fsdp")

    def natural(part):
        return part.reshape(outer, inner, rows, -1).swapaxes(0, 1).reshape(width, -1).astype(F32)

    def cut(part, sizes):
        found, at = [], 0
        for size in sizes:
            found.append(part[:, at : at + size])
            at += size
        return found

    dense = [width, hidden, hidden, 128]
    wq0, block_c = cut(natural(sent_c), [3 * width, 128])
    wq1, wo0, wi0, wf0, block_b = cut(natural(sent_b), [3 * width] + dense)
    wo1, wi1, wf1, block_a = cut(natural(sent_a), dense)

    def vectors(block):
        block = block.reshape(DEVICES, rows, 128)
        return block[:, :, :rows].swapaxes(0, 1).reshape(rows, width)

    def line(block):
        block = block.reshape(DEVICES, rows, 128)
        return block[:, 0, 2 * rows : 2 * rows + hidden // DEVICES].reshape(-1)

    def stacked(part):
        part = part.reshape(DEVICES, rows, -1, width).swapaxes(1, 2)
        return part.reshape(hidden, width)

    def spread(parts, axis):
        return lax.psum_scatter(jnp.stack(parts), axes, scatter_dimension=axis, tiled=True)

    return (
        spread([wq0, wq1], 1),
        spread([vectors(block_c)[0:2], vectors(block_b)[0:2]], 2),
        spread([wo0, wo1], 1),
        spread([wi0, wi1], 1),
        spread([line(block_b), line(block_a)], 1),
        spread([stacked(wf0), stacked(wf1)], 1),
        spread([vectors(block_b)[2:4], vectors(block_a)[2:4]], 2),
        spread([vectors(block_b)[4:8], vectors(block_a)[4:8]], 2),
    )


def solution(mesh):
    placed = (
        P(("dp", "fsdp"), None),
        P(("dp", "fsdp"), None),
        P(("dp", "fsdp"), None),
        P(None, ("dp", "fsdp"), None),
        P(None, None, ("dp", "fsdp")),
        P(None, ("dp", "fsdp"), None),
        P(None, ("dp", "fsdp"), None),
        P(None, ("dp", "fsdp")),
        P(None, ("dp", "fsdp"), None),
        P(None, None, ("dp", "fsdp")),
        P(None, None, ("dp", "fsdp")),
    )
    return jax.shard_map(
        local,
        mesh=mesh,
        in_specs=placed,
        out_specs=(
            P(("dp", "fsdp"), None),
            P(("dp", "fsdp"), None),
            P(None, ("dp", "fsdp"), None),
            P(None, None, ("dp", "fsdp")),
            P(None, ("dp", "fsdp"), None),
            P(None, ("dp", "fsdp"), None),
            P(None, ("dp", "fsdp")),
            P(None, ("dp", "fsdp"), None),
            P(None, None, ("dp", "fsdp")),
            P(None, None, ("dp", "fsdp")),
        ),
        check_vma=False,
    )
```

profile of v0, /device:TPU:0, one launch (start us, length us, event | category | flops | bytes accessed | tf_op | source)
XLA Modules:
  0.0 164.8 jit_solution(12668905762651164491)
XLA Ops:
  0.6 1.8 %shard_map.187 = (bf16[64,3968]{1,0:T(8,128)(2,1)}, bf16[64,2304]{1,0:T(8,128)(2,1)}) custom-call(bf16[2,8,768]{2,1,0:T(8,128)(2,1)} %wq_ref.1, bf16[2,2,8]{2,1,0:T(2,128)(2,1)} %ab_ref.1, bf16[2,8,256]{2,1,0:T(8,128)(2,1)} %wo_ref.1, bf16[2,8,1024]{2,1,0:T(8,128)(2,1)} %wi_ref.1, bf16[2,32]{1,0:T(2,128)(2,1)} %bi_ref.1, bf16[2,32,256]{2,1,0:T(8,128)(2,1)} %wf_ref.1, ...), custom_call_target="tpu_custom_call" | custom-call | tf_op jit(solution)/shard_map/pallas_call | solution.py:883
  2.4 7.3 %all-to-all-start = ((bf16[8,8,3968]{2,1,0:T(8,128)(2,1)}), bf16[8,8,3968]{2,1,0:T(8,128)(2,1)}, u32[]{:S(2)}, u32[]{:S(2)}) async-start(bf16[8,8,3968]{2,1,0:T(8,128)(2,1)} %bitcast.7), calls=%async_computation | async-start | bytes 1015808 | tf_op jit(solution)/shard_map/all_to_all | solution.py:1010
  9.7 4.6 %shard_map.186 = (bf16[2048,256]{1,0:T(8,128)(2,1)}, bf16[2048,256]{1,0:T(8,128)(2,1)}) custom-call(s32[4,6]{1,0:T(4,128)} %lengths_ref.17, bf16[2048,256]{1,0:T(8,128)(2,1)} %refs_0_.1, bf16[2048,256]{1,0:T(8,128)(2,1)} %refs_1_.1), custom_call_target="tpu_custom_call" | custom-call | flops 1000000 | bytes 8388608 | tf_op jit(solution)/shard_map/pallas_call | solution.py:504
  14.3 9.6 %all-to-all-done = bf16[8,8,3968]{2,1,0:T(8,128)(2,1)} async-done(((bf16[8,8,3968]{2,1,0:T(8,128)(2,1)}), bf16[8,8,3968]{2,1,0:T(8,128)(2,1)}, u32[]{:S(2)}, u32[]{:S(2)}) %all-to-all-start) | async-done | bytes 507936 | tf_op jit(solution)/shard_map/all_to_all | solution.py:1010
  24.9 1.6 collective-permute-start.1
  26.8 1.8 %slice.9.refs_4_.refs_3_.refs_17_ = bf16[64,3072]{1,0:T(8,128)(2,1)} slice(bf16[64,3968]{1,0:T(8,128)(2,1)} %shard_map.188), slice={[0:64], [896:3968]} | slice | bytes 786432 | tf_op jit(solution)/shard_map/slice | solution.py:1047
  28.5 1.5 collective-permute-start.4
  30.3 2.6 %collective-permute-done.1.refs_4_ = bf16[64,896]{1,0:T(8,128)(2,1)S(1)} collective-permute-done((bf16[64,896]{1,0:T(8,128)(2,1)S(1)}, bf16[64,896]{1,0:T(8,128)(2,1)S(1)}, u32[]{:S(2)}, u32[]{:S(2)}) %collective-permute-start.1) | collective-permute-done | bytes 114720 | tf_op jit(solution)/shard_map/ppermute | solution.py:1015
  34.2 7.6 %shard_map.189 = (bf16[4,4,128,512]{3,2,1,0:T(8,128)(2,1)}, bf16[4,4,128,512]{3,2,1,0:T(8,128)(2,1)}, bf16[4,4,80,512]{3,2,1,0:T(8,128)(2,1)}, bf16[4,256,512]{2...) custom-call(s32[4,6]{1,0:T(4,128)} %lengths_ref.17, s32[1]{0:T(128)} %bitcast.refs_0_, ...), custom_call_target="tpu_custom_call" | custom-call | flops 4000000000 | bytes 8388608 | tf_op jit(solution)/shard_map/pallas_call | solution.py:504
  41.9 4.3 %all-to-all-start.1 = ((bf16[8,8,2304]{2,1,0:T(8,128)(2,1)}), bf16[8,8,2304]{2,1,0:T(8,128)(2,1)}, u32[]{:S(2)}, u32[]{:S(2)}) async-start(bf16[8,8,2304]{2,1,0:T(8,128)(2,1)} %bitcast.6), calls=%async_computation.1 | async-start | bytes 589824 | tf_op jit(solution)/shard_map/all_to_all | solution.py:1010
  46.2 11.4 %shard_map.191 = (f32[2048,256]{1,0:T(8,128)}, f32[2048,256]{1,0:T(8,128)}, f32[2048,128]{1,0:T(8,128)}, bf16[2048,256]{1,0:T(8,128)(2,1)}, bf16[2048,1024]{1,0:...) custom-call(s32[4,6]{1,0:T(4,128)} %lengths_ref.17, s32[1]{0:T(128)} %bitcast.refs_0_, ...), custom_call_target="tpu_custom_call" | custom-call | flops 5000000000 | bytes 8388608 | tf_op jit(solution)/shard_map/pallas_call | solution.py:504
  57.6 1.1 collective-permute-start.7
  58.7 8.3 %shard_map.192 = (bf16[4,4,128,512]{3,2,1,0:T(8,128)(2,1)}, bf16[4,4,128,512]{3,2,1,0:T(8,128)(2,1)}, bf16[4,4,80,512]{3,2,1,0:T(8,128)(2,1)}, bf16[4,256,512]{2,1,0:T(8,128)(2,1)}, f32[4,8,512]{2,1,0:T(8,128)}) custom-call(s32[4,6]{1,0:T(4,128)} %lengths_ref.17, s32[1]{0:T(128)} %bitcast.refs_0_, f32[2048,256]{1,0:T(8,128)} %get-tuple-element.72.refs_1_, ...), custom_call_target="tpu_custom_call" | custom-call | flops 4000000000 | bytes 8388608 | tf_op jit(solution)/shard_map/pallas_call | solution.py:504
  67.5 1.8 %collective-permute-done.8.refs_8_ = bf16[64,2304]{1,0:T(8,128)(2,1)} collective-permute-done((bf16[64,2304]{1,0:T(8,128)(2,1)}, bf16[64,2304]{1,0:T(8,128)(2,1)}, u32[]{:S(2)}, u32[]{:S(2)}) %collective-permute-start.8) | collective-permute-done | bytes 294944 | tf_op jit(solution)/shard_map/ppermute | solution.py:1015
  69.3 18.9 %shard_map.196 = (bf16[2048,256]{1,0:T(8,128)(2,1)}, f32[2048,256]{1,0:T(8,128)}, bf16[4,256,512]{2,1,0:T(8,128)(2,1)}, bf16[64,2432]{1,0:T(8,128)(2,1)}, bf16[6...) custom-call(s32[4,6]{1,0:T(4,128)} %lengths_ref.17, s32[1]{0:T(128)} %bitcast.refs_0_, ...), custom_call_target="tpu_custom_call" | custom-call | flops 10000000000 | bytes 8388608 | tf_op jit(solution)/shard_map/pallas_call | solution.py:504
  90.2 21.7 %shard_map.197 = (f32[2048,256]{1,0:T(8,128)}, bf16[4,256,512]{2,1,0:T(8,128)(2,1)}, bf16[64,3200]{1,0:T(8,128)(2,1)}, bf16[64,3200]{1,0:T(8,128)(2,1)}, bf16[64...) custom-call(s32[4,6]{1,0:T(4,128)} %lengths_ref.17, s32[1]{0:T(128)} %bitcast.refs_0_, ...), custom_call_target="tpu_custom_call" | custom-call | flops 15000000512 | bytes 8388608 | tf_op jit(solution)/shard_map/pallas_call | solution.py:504
  113.8 2.1 %shard_map.198 = (bf16[32,2432]{1,0:T(8,128)(2,1)}, bf16[32,2432]{1,0:T(8,128)(2,1)}) custom-call(s32[1]{0:T(128)} %bitcast.5.place_ref, bf16[64,2432]{1,0:T(8,128)(2,1)} %get-tuple-element.77.refs_21_.refs_0_, bf16[64,2432]{1,0:T(8,128)(2,1)} %collective-permute-done.9.refs_1_, bf16[64,2432]{1,0:T(8,128)(2,1)} %collective-permute-done.10.refs_2_, ...), custom_call_target="tpu_custom_call" | custom-call | tf_op jit(solution)/shard_map/pallas_call | solution.py:919
  115.9 2.0 %collective-permute-start.12 = (bf16[32,2432]{1,0:T(8,128)(2,1)}, bf16[32,2432]{1,0:T(8,128)(2,1)}, u32[]{:S(2)}, u32[]{:S(2)}) collective-permute-start(bf16[32,2432]{1,0:T(8,128)(2,1)} %get-tuple-element.95), channel_id=1, source_target_pairs={{0,4},{4,0},{8,12},{12,8},{16,20},{20,16},{24,28},{28,24},{1,5},{5... | collective-permute-start | bytes 466952 | tf_op jit(solution)/shard_map/ppermute | solution.py:1015
  118.0 10.5 %shard_map.199 = (bf16[4,768,512]{2,1,0:T(8,128)(2,1)}, bf16[64,896]{1,0:T(8,128)(2,1)}, bf16[64,896]{1,0:T(8,128)(2,1)}, bf16[64,896]{1,0:T(8,128)(2,1)}, bf16[64,896]{1,0:T(8,128)(2,1)}) custom-call(s32[4,6]{1,0:T(4,128)} %lengths_ref.17, s32[1]{0:T(128)} %bitcast.refs_0_, bf16[2048,256]{1,0:T(8,128)(2,1)} %get-tuple-element.68.refs_1_, ...), custom_call_target="tpu_custom_call" | custom-call | flops 8000000000 | bytes 8388608 | tf_op jit(solution)/shard_map/pallas_call | solution.py:504
  130.4 1.9 %collective-permute-done.15.refs_3_ = bf16[64,3200]{1,0:T(8,128)(2,1)} collective-permute-done((bf16[64,3200]{1,0:T(8,128)(2,1)}, bf16[64,3200]{1,0:T(8,128)(2,1)}, u32[]{:S(2)}, u32[]{:S(2)}) %collective-permute-start.15) | collective-permute-done | bytes 409632 | tf_op jit(solution)/shard_map/ppermute | solution.py:1015
  132.3 2.4 %shard_map.200 = (bf16[32,3200]{1,0:T(8,128)(2,1)}, bf16[32,3200]{1,0:T(8,128)(2,1)}) custom-call(s32[1]{0:T(128)} %bitcast.5.place_ref, bf16[64,3200]{1,0:T(8,128)(2,1)} %get-tuple-element.93.refs_4_.refs_8_.refs_0_, bf16[64,3200]{1,0:T(8,128)(2,1)} %collective-permute-done.13.refs_1_, bf16[64,3200]{1,0:T(8,128)(2,1)} %collective-permute-done.14.refs_2_, ...), custom_call_target="tpu_custom_call" | custom-call | tf_op jit(solution)/shard_map/pallas_call | solution.py:919
  134.7 1.6 collective-permute-done.18.refs_2_
  136.9 1.8 %shard_map.201 = (bf16[32,896]{1,0:T(8,128)(2,1)}, bf16[32,896]{1,0:T(8,128)(2,1)}) custom-call(s32[1]{0:T(128)} %bitcast.5.place_ref, bf16[64,896]{1,0:T(8,128)(2,1)} %get-tuple-element.107.refs_0_, bf16[64,896]{1,0:T(8,128)(2,1)} %collective-permute-done.17.refs_1_, bf16[64,896]{1,0:T(8,128)(2,1)} %collective-permute-done.18.refs_2_, ...), custom_call_target="tpu_custom_call" | custom-call | tf_op jit(solution)/shard_map/pallas_call | solution.py:919
  138.7 2.0 %collective-permute-start.20 = (bf16[32,896]{1,0:T(8,128)(2,1)}, bf16[32,896]{1,0:T(8,128)(2,1)}, u32[]{:S(2)}, u32[]{:S(2)}) collective-permute-start(bf16[32,896]{1,0:T(8,128)(2,1)} %get-tuple-element.112), channel_id=1, source_target_pairs={{0,4},{4,0},{8,12},{12,8},{16,20},{20,16},{24,28},{28,24},{1,5},{5... | collective-permute-start | bytes 172040 | tf_op jit(solution)/shard_map/ppermute | solution.py:1015
  140.8 5.4 %shard_map.202.refs_6_ = bf16[2048,256]{1,0:T(8,128)(2,1)} custom-call(s32[4,6]{1,0:T(4,128)} %lengths_ref.17, bf16[4,768,512]{2,1,0:T(8,128)(2,1)} %get-tuple-element.104.refs_5_.refs_0_, f32[2048,256]{1,0:T(8,128)} %get-tuple-element.113.refs_1_, bf16[4,64,896]{2,1,0:T(8,128)(2,1)} %get-tuple-element.71.refs_3_.refs_2_.refs_4_.refs_16_, ...), custom_call_target="tpu_custom_call" | custom-call | flops 10000000000 | bytes 8388608 | tf_op jit(solution)/shard_map/pallas_call | solution.py:504
  146.2 2.3 %collective-permute-done.16.refs_3_ = bf16[32,3200]{1,0:T(8,128)(2,1)} collective-permute-done((bf16[32,3200]{1,0:T(8,128)(2,1)}, bf16[32,3200]{1,0:T(8,128)(2,1)}, u32[]{:S(2)}, u32[]{:S(2)}) %collective-permute-start.16) | collective-permute-done | bytes 204832 | tf_op jit(solution)/shard_map/ppermute | solution.py:1015
  148.5 2.0 %shard_map.203 = (bf16[8,6528]{1,0:T(8,128)(2,1)}, bf16[8,6528]{1,0:T(8,128)(2,1)}, bf16[8,6528]{1,0:T(8,128)(2,1)}, bf16[8,6528]{1,0:T(8,128)(2,1)}) custom-call(s32[1]{0:T(128)} %bitcast.5.place_ref, bf16[32,2432]{1,0:T(8,128)(2,1)} %get-tuple-element.94.refs_9_.refs_0_, bf16[32,2432]{1,0:T(8,128)(2,1)} %collective-permute-done.12.refs_4_.refs_1_, ...), custom_call_target="tpu_custom_call" | custom-call | tf_op jit(solution)/shard_map/pallas_call | solution.py:948
  150.5 1.5 collective-permute-start.21
  152.0 2.4 %collective-permute-start.22 = (bf16[8,6528]{1,0:T(8,128)(2,1)}, bf16[8,6528]{1,0:T(8,128)(2,1)}, u32[]{:S(2)}, u32[]{:S(2)}) collective-permute-start(bf16[8,6528]{1,0:T(8,128)(2,1)} %get-tuple-element.116), channel_id=1, source_target_pairs={{0,16},{4,20},{8,24},{12,28},{16,0},{20,4},{24,8},{28,12},{1,17},{... | collective-permute-start | bytes 313352 | tf_op jit(solution)/shard_map/ppermute | solution.py:1015
  154.9 3.9 %shard_map.204.refs_4_ = bf16[2048,256]{1,0:T(8,128)(2,1)} custom-call(s32[4,6]{1,0:T(4,128)} %lengths_ref.17, bf16[2048,256]{1,0:T(8,128)(2,1)} %get-tuple-element.76.refs_0_, bf16[8,6528]{1,0:T(8,128)(2,1)} %get-tuple-element.114.refs_1_.refs_0_), custom_call_target="tpu_custom_call" | custom-call | flops 3000000000 | bytes 8388608 | tf_op jit(solution)/shard_map/pallas_call | solution.py:504
  158.8 4.3 %collective-permute-done.22.refs_2_ = bf16[8,6528]{1,0:T(8,128)(2,1)} collective-permute-done((bf16[8,6528]{1,0:T(8,128)(2,1)}, bf16[8,6528]{1,0:T(8,128)(2,1)}, u32[]{:S(2)}, u32[]{:S(2)}) %collective-permute-start.22) | collective-permute-done | bytes 104480 | tf_op jit(solution)/shard_map/ppermute | solution.py:1015
  163.1 1.7 %shard_map.205 = (f32[2,8,768]{2,1,0:T(8,128)}, f32[2,2,8]{2,1,0:T(2,128)}, f32[2,8,256]{2,1,0:T(8,128)}, f32[2,8,1024]{2,1,0:T(8,128)}, f32[2,32]{1,0:T(2,128)}...) custom-call(bf16[8,6528]{1,0:T(8,128)(2,1)} %get-tuple-element.114.refs_1_.refs_0_, ...), custom_call_target="tpu_custom_call" | custom-call | tf_op jit(solution)/shard_map/pallas_call | solution.py:1000
  (50 shorter events, 10.5 us)
Async XLA Ops:
  2.4 21.5 %all-to-all-start = ((bf16[8,8,3968]{2,1,0:T(8,128)(2,1)}), bf16[8,8,3968]{2,1,0:T(8,128)(2,1)}, u32[]{:S(2)}, u32[]{:S(2)}) async-start(bf16[8,8,3968]{2,1,0:T(8,128)(2,1)} %bitcast.7), calls=%async_computation | async-start | bytes 1015808 | tf_op jit(solution)/shard_map/all_to_all | solution.py:1010
  24.8 1.7 %copy-start = (bf16[64,896]{1,0:T(8,128)(2,1)}, bf16[64,896]{1,0:T(8,128)(2,1)S(1)}, u32[]{:S(2)}) copy-start(bf16[64,896]{1,0:T(8,128)(2,1)S(1)} %slice.8.refs_2_) | copy-start | bytes 344068
  24.8 5.4 %collective-permute-start.2 = (bf16[64,896]{1,0:T(8,128)(2,1)S(1)}, bf16[64,896]{1,0:T(8,128)(2,1)S(1)}, u32[]{:S(2)}, u32[]{:S(2)}) collective-permute-start(bf16[64,896]{1,0:T(8,128)(2,1)S(1)} %slice.8.refs_2_), channel_id=1, source_target_pairs={{0,3},{1,2},{2,1},{3,0},{4,7},{5,6},{6,5},{7,4},{8,11},{9,10},{10,... | collective-permute-start | bytes 344072 | tf_op jit(solution)/shard_map/ppermute | solution.py:1015
  24.9 8.0 %collective-permute-start.1 = (bf16[64,896]{1,0:T(8,128)(2,1)S(1)}, bf16[64,896]{1,0:T(8,128)(2,1)S(1)}, u32[]{:S(2)}, u32[]{:S(2)}) collective-permute-start(bf16[64,896]{1,0:T(8,128)(2,1)S(1)} %slice.8.refs_2_), channel_id=1, source_target_pairs={{0,2},{1,3},{2,0},{3,1},{4,6},{5,7},{6,4},{7,5},{8,10},{9,11},{10,... | collective-permute-start | bytes 344072 | tf_op jit(solution)/shard_map/ppermute | solution.py:1015
  26.5 6.4 %collective-permute-start = (bf16[64,896]{1,0:T(8,128)(2,1)S(1)}, bf16[64,896]{1,0:T(8,128)(2,1)S(1)}, u32[]{:S(2)}, u32[]{:S(2)}) collective-permute-start(bf16[64,896]{1,0:T(8,128)(2,1)S(1)} %slice.8.refs_2_), channel_id=1, source_target_pairs={{0,1},{1,0},{2,3},{3,2},{4,5},{5,4},{6,7},{7,6},{8,9},{9,8},{10,11... | collective-permute-start | bytes 344072 | tf_op jit(solution)/shard_map/ppermute | solution.py:1015
  28.5 13.2 %collective-permute-start.4 = (bf16[64,3072]{1,0:T(8,128)(2,1)}, bf16[64,3072]{1,0:T(8,128)(2,1)}, u32[]{:S(2)}, u32[]{:S(2)}) collective-permute-start(bf16[64,3072]{1,0:T(8,128)(2,1)} %slice.9.refs_4_.refs_3_.refs_17_), channel_id=1, source_target_pairs={{0,2},{1,3},{2,0},{3,1},{4,6},{5,7},{6,4},{7,5},{8,10},{9,11},{10,... | collective-permute-start | bytes 1179656 | tf_op jit(solution)/shard_map/ppermute | solution.py:1015
  30.1 16.1 %collective-permute-start.3 = (bf16[64,3072]{1,0:T(8,128)(2,1)}, bf16[64,3072]{1,0:T(8,128)(2,1)}, u32[]{:S(2)}, u32[]{:S(2)}) collective-permute-start(bf16[64,3072]{1,0:T(8,128)(2,1)} %slice.9.refs_4_.refs_3_.refs_17_), channel_id=1, source_target_pairs={{0,1},{1,0},{2,3},{3,2},{4,5},{5,4},{6,7},{7,6},{8,9},{9,8},{10,11... | collective-permute-start | bytes 1179656 | tf_op jit(solution)/shard_map/ppermute | solution.py:1015
  30.3 2.6 %copy-start.1 = (bf16[64,896]{1,0:T(8,128)(2,1)}, bf16[64,896]{1,0:T(8,128)(2,1)S(1)}, u32[]{:S(2)}) copy-start(bf16[64,896]{1,0:T(8,128)(2,1)S(1)} %collective-permute-done.2.refs_5_) | copy-start | bytes 344068
  32.9 0.6 copy-start.2
  33.5 0.6 copy-start.3
  41.8 4.4 %collective-permute-start.5 = (bf16[64,3072]{1,0:T(8,128)(2,1)}, bf16[64,3072]{1,0:T(8,128)(2,1)}, u32[]{:S(2)}, u32[]{:S(2)}) collective-permute-start(bf16[64,3072]{1,0:T(8,128)(2,1)} %shard_map.190.refs_6_.refs_5_.refs_19_), channel_id=1, source_target_pairs={{0,1},{1,0},{2,3},{3,2},{4,5},{5,4},{6,7},{7,6},{8,9},{9,8},{10,11... | collective-permute-start | bytes 1179656 | tf_op jit(solution)/shard_map/ppermute | solution.py:1015
  41.9 15.7 %all-to-all-start.1 = ((bf16[8,8,2304]{2,1,0:T(8,128)(2,1)}), bf16[8,8,2304]{2,1,0:T(8,128)(2,1)}, u32[]{:S(2)}, u32[]{:S(2)}) async-start(bf16[8,8,2304]{2,1,0:T(8,128)(2,1)} %bitcast.6), calls=%async_computation.1 | async-start | bytes 589824 | tf_op jit(solution)/shard_map/all_to_all | solution.py:1010
  57.6 9.8 %collective-permute-start.7 = (bf16[64,2304]{1,0:T(8,128)(2,1)}, bf16[64,2304]{1,0:T(8,128)(2,1)}, u32[]{:S(2)}, u32[]{:S(2)}) collective-permute-start(bf16[64,2304]{1,0:T(8,128)(2,1)} %shard_map.194.refs_5_), channel_id=1, source_target_pairs={{0,2},{1,3},{2,0},{3,1},{4,6},{5,7},{6,4},{7,5},{8,10},{9,11},{10,... | collective-permute-start | bytes 884744 | tf_op jit(solution)/shard_map/ppermute | solution.py:1015
  58.7 8.8 %collective-permute-start.6 = (bf16[64,2304]{1,0:T(8,128)(2,1)}, bf16[64,2304]{1,0:T(8,128)(2,1)}, u32[]{:S(2)}, u32[]{:S(2)}) collective-permute-start(bf16[64,2304]{1,0:T(8,128)(2,1)} %shard_map.194.refs_5_), channel_id=1, source_target_pairs={{0,1},{1,0},{2,3},{3,2},{4,5},{5,4},{6,7},{7,6},{8,9},{9,8},{10,11... | collective-permute-start | bytes 884744 | tf_op jit(solution)/shard_map/ppermute | solution.py:1015
  67.3 1.9 %collective-permute-start.8 = (bf16[64,2304]{1,0:T(8,128)(2,1)}, bf16[64,2304]{1,0:T(8,128)(2,1)}, u32[]{:S(2)}, u32[]{:S(2)}) collective-permute-start(bf16[64,2304]{1,0:T(8,128)(2,1)} %shard_map.195.refs_7_), channel_id=1, source_target_pairs={{0,1},{1,0},{2,3},{3,2},{4,5},{5,4},{6,7},{7,6},{8,9},{9,8},{10,11... | collective-permute-start | bytes 884744 | tf_op jit(solution)/shard_map/ppermute | solution.py:1015
  88.2 25.1 %collective-permute-start.9 = (bf16[64,2432]{1,0:T(8,128)(2,1)}, bf16[64,2432]{1,0:T(8,128)(2,1)}, u32[]{:S(2)}, u32[]{:S(2)}) collective-permute-start(bf16[64,2432]{1,0:T(8,128)(2,1)} %get-tuple-element.78), channel_id=1, source_target_pairs={{0,1},{1,0},{2,3},{3,2},{4,5},{5,4},{6,7},{7,6},{8,9},{9,8},{10,11... | collective-permute-start | bytes 933896 | tf_op jit(solution)/shard_map/ppermute | solution.py:1015
  88.5 25.3 %collective-permute-start.10 = (bf16[64,2432]{1,0:T(8,128)(2,1)}, bf16[64,2432]{1,0:T(8,128)(2,1)}, u32[]{:S(2)}, u32[]{:S(2)}) collective-permute-start(bf16[64,2432]{1,0:T(8,128)(2,1)} %get-tuple-element.79), channel_id=1, source_target_pairs={{0,2},{1,3},{2,0},{3,1},{4,6},{5,7},{6,4},{7,5},{8,10},{9,11},{10,... | collective-permute-start | bytes 933896 | tf_op jit(solution)/shard_map/ppermute | solution.py:1015
  89.5 24.3 %collective-permute-start.11 = (bf16[64,2432]{1,0:T(8,128)(2,1)}, bf16[64,2432]{1,0:T(8,128)(2,1)}, u32[]{:S(2)}, u32[]{:S(2)}) collective-permute-start(bf16[64,2432]{1,0:T(8,128)(2,1)} %get-tuple-element.80), channel_id=1, source_target_pairs={{0,3},{1,2},{2,1},{3,0},{4,7},{5,6},{6,5},{7,4},{8,11},{9,10},{10,... | collective-permute-start | bytes 933896 | tf_op jit(solution)/shard_map/ppermute | solution.py:1015
  111.9 17.1 %collective-permute-start.13 = (bf16[64,3200]{1,0:T(8,128)(2,1)}, bf16[64,3200]{1,0:T(8,128)(2,1)}, u32[]{:S(2)}, u32[]{:S(2)}) collective-permute-start(bf16[64,3200]{1,0:T(8,128)(2,1)} %get-tuple-element.96), channel_id=1, source_target_pairs={{0,1},{1,0},{2,3},{3,2},{4,5},{5,4},{6,7},{7,6},{8,9},{9,8},{10,11... | collective-permute-start | bytes 1228808 | tf_op jit(solution)/shard_map/ppermute | solution.py:1015
  112.4 17.3 %collective-permute-start.14 = (bf16[64,3200]{1,0:T(8,128)(2,1)}, bf16[64,3200]{1,0:T(8,128)(2,1)}, u32[]{:S(2)}, u32[]{:S(2)}) collective-permute-start(bf16[64,3200]{1,0:T(8,128)(2,1)} %get-tuple-element.97), channel_id=1, source_target_pairs={{0,2},{1,3},{2,0},{3,1},{4,6},{5,7},{6,4},{7,5},{8,10},{9,11},{10,... | collective-permute-start | bytes 1228808 | tf_op jit(solution)/shard_map/ppermute | solution.py:1015
  113.4 18.9 %collective-permute-start.15 = (bf16[64,3200]{1,0:T(8,128)(2,1)}, bf16[64,3200]{1,0:T(8,128)(2,1)}, u32[]{:S(2)}, u32[]{:S(2)}) collective-permute-start(bf16[64,3200]{1,0:T(8,128)(2,1)} %get-tuple-element.98), channel_id=1, source_target_pairs={{0,3},{1,2},{2,1},{3,0},{4,7},{5,6},{6,5},{7,4},{8,11},{9,10},{10,... | collective-permute-start | bytes 1228808 | tf_op jit(solution)/shard_map/ppermute | solution.py:1015
  115.9 16.3 %collective-permute-start.12 = (bf16[32,2432]{1,0:T(8,128)(2,1)}, bf16[32,2432]{1,0:T(8,128)(2,1)}, u32[]{:S(2)}, u32[]{:S(2)}) collective-permute-start(bf16[32,2432]{1,0:T(8,128)(2,1)} %get-tuple-element.95), channel_id=1, source_target_pairs={{0,4},{4,0},{8,12},{12,8},{16,20},{20,16},{24,28},{28,24},{1,5},{5... | collective-permute-start | bytes 466952 | tf_op jit(solution)/shard_map/ppermute | solution.py:1015
  128.4 6.2 %collective-permute-start.17 = (bf16[64,896]{1,0:T(8,128)(2,1)}, bf16[64,896]{1,0:T(8,128)(2,1)}, u32[]{:S(2)}, u32[]{:S(2)}) collective-permute-start(bf16[64,896]{1,0:T(8,128)(2,1)} %get-tuple-element.108), channel_id=1, source_target_pairs={{0,1},{1,0},{2,3},{3,2},{4,5},{5,4},{6,7},{7,6},{8,9},{9,8},{10,11... | collective-permute-start | bytes 344072 | tf_op jit(solution)/shard_map/ppermute | solution.py:1015
  128.9 7.3 %collective-permute-start.18 = (bf16[64,896]{1,0:T(8,128)(2,1)}, bf16[64,896]{1,0:T(8,128)(2,1)}, u32[]{:S(2)}, u32[]{:S(2)}) collective-permute-start(bf16[64,896]{1,0:T(8,128)(2,1)} %get-tuple-element.109), channel_id=1, source_target_pairs={{0,2},{1,3},{2,0},{3,1},{4,6},{5,7},{6,4},{7,5},{8,10},{9,11},{10,... | collective-permute-start | bytes 344072 | tf_op jit(solution)/shard_map/ppermute | solution.py:1015
  129.6 7.3 %collective-permute-start.19 = (bf16[64,896]{1,0:T(8,128)(2,1)}, bf16[64,896]{1,0:T(8,128)(2,1)}, u32[]{:S(2)}, u32[]{:S(2)}) collective-permute-start(bf16[64,896]{1,0:T(8,128)(2,1)} %get-tuple-element.110), channel_id=1, source_target_pairs={{0,3},{1,2},{2,1},{3,0},{4,7},{5,6},{6,5},{7,4},{8,11},{9,10},{10,... | collective-permute-start | bytes 344072 | tf_op jit(solution)/shard_map/ppermute | solution.py:1015
  138.7 7.5 %collective-permute-start.20 = (bf16[32,896]{1,0:T(8,128)(2,1)}, bf16[32,896]{1,0:T(8,128)(2,1)}, u32[]{:S(2)}, u32[]{:S(2)}) collective-permute-start(bf16[32,896]{1,0:T(8,128)(2,1)} %get-tuple-element.112), channel_id=1, source_target_pairs={{0,4},{4,0},{8,12},{12,8},{16,20},{20,16},{24,28},{28,24},{1,5},{5... | collective-permute-start | bytes 172040 | tf_op jit(solution)/shard_map/ppermute | solution.py:1015
  140.7 7.7 %collective-permute-start.16 = (bf16[32,3200]{1,0:T(8,128)(2,1)}, bf16[32,3200]{1,0:T(8,128)(2,1)}, u32[]{:S(2)}, u32[]{:S(2)}) collective-permute-start(bf16[32,3200]{1,0:T(8,128)(2,1)} %get-tuple-element.106), channel_id=1, source_target_pairs={{0,4},{4,0},{8,12},{12,8},{16,20},{20,16},{24,28},{28,24},{1,5},{5... | collective-permute-start | bytes 614408 | tf_op jit(solution)/shard_map/ppermute | solution.py:1015
  150.5 8.3 %collective-permute-start.21 = (bf16[8,6528]{1,0:T(8,128)(2,1)}, bf16[8,6528]{1,0:T(8,128)(2,1)}, u32[]{:S(2)}, u32[]{:S(2)}) collective-permute-start(bf16[8,6528]{1,0:T(8,128)(2,1)} %get-tuple-element.115), channel_id=1, source_target_pairs={{0,8},{4,12},{8,0},{12,4},{16,24},{20,28},{24,16},{28,20},{1,9},{5... | collective-permute-start | bytes 313352 | tf_op jit(solution)/shard_map/ppermute | solution.py:1015
  152.0 11.0 %collective-permute-start.22 = (bf16[8,6528]{1,0:T(8,128)(2,1)}, bf16[8,6528]{1,0:T(8,128)(2,1)}, u32[]{:S(2)}, u32[]{:S(2)}) collective-permute-start(bf16[8,6528]{1,0:T(8,128)(2,1)} %get-tuple-element.116), channel_id=1, source_target_pairs={{0,16},{4,20},{8,24},{12,28},{16,0},{20,4},{24,8},{28,12},{1,17},{... | collective-permute-start | bytes 313352 | tf_op jit(solution)/shard_map/ppermute | solution.py:1015
  154.4 8.7 %collective-permute-start.23 = (bf16[8,6528]{1,0:T(8,128)(2,1)}, bf16[8,6528]{1,0:T(8,128)(2,1)}, u32[]{:S(2)}, u32[]{:S(2)}) collective-permute-start(bf16[8,6528]{1,0:T(8,128)(2,1)} %get-tuple-element.117), channel_id=1, source_target_pairs={{0,24},{4,28},{8,16},{12,20},{16,8},{20,12},{24,0},{28,4},{1,25},{... | collective-permute-start | bytes 313352 | tf_op jit(solution)/shard_map/ppermute | solution.py:1015
where the time goes:
time: 166 us; the launch traced here: 165 us
  Pallas kernels  104 us (63%)
  starting transfers between devices  30.5 us (18%)
  waiting for transfers between devices  25.4 us (15%)
  local copies, waits for them, and re-layouts  3.96 us (2%)
    pallas_call x9, Pallas kernels, run_rows(): pl.pallas_call(kernel, grid=(count // group,), in_specs=[pl.BlockSpec(mem...  92.3 us
    ppermute x24, starting transfers between devices, swap(): lax.ppermute(part, axis, [(source, source ^ step) for source in range(siz...  19 us
    ppermute x24, waiting for transfers between devices, swap(): lax.ppermute(part, axis, [(source, source ^ step) for source in range(siz...  15.8 us
    all_to_all x2, starting transfers between devices, exchange(): return lax.all_to_all(parts, axis, 0, 0, tiled=True)  11.5 us
    all_to_all x2, waiting for transfers between devices, exchange(): return lax.all_to_all(parts, axis, 0, 0, tiled=True)  9.63 us
    pallas_call x3, Pallas kernels, add_parts(): pl.pallas_call(kernel, in_specs=[pl.BlockSpec(memory_space=pltpu.SMEM)] +...  6.28 us
  transfers between devices with their start and end apart: 26, of which 10 were waited for; matrix products, arithmetic and copies ran while one was open for 1% of the time, Pallas kernels for 47%

commit v1 on v0

--- a/solution.py
+++ b/solution.py
@@ -463,12 +463,16 @@
 
 def run_rows(
     body, lengths, rowwise, fixed, row_outs, sent, shared, private, cost, setup, finish, after=(),
-    scalars=(), group=1
+    scalars=(), group=1, late=()
 ):
     count = lengths.shape[0]
     group = group if count % group == 0 else 1
-    cuts = [len(scalars), len(rowwise), len(fixed), len(after), len(row_outs), len(sent)]
-    cuts += [len(shared)] + [len(private)] * group
+    cuts = [len(scalars), len(rowwise), len(fixed), len(after), len(late), len(row_outs), len(sent)]
+    cuts += [len(shared)] + [len(private)] * group + [len(late), 1 if late else 0]
+    late_blocks = [
+        (group * SEQ, part.shape[1]) if len(part.shape) == 2 else (group,) + tuple(part.shape[1:])
+        for part in late
+    ]
 
     def kernel(lengths_ref, *refs):
         step = pl.program_id(0)
@@ -477,7 +481,21 @@
         for cut in cuts:
             groups.append(refs[at : at + cut])
             at += cut
-        numbers, rows_in, fixed_in, unused, rows_out, sent_out, work = groups[:7]
+        numbers, rows_in, fixed_in, unused, late_in, rows_out, sent_out, work = groups[:8]
+        late_refs = groups[8 + group]
+        copies = [
+            pltpu.make_async_copy(
+                source.at[pl.ds(step * block[0], block[0])], target, groups[-1][0].at[index]
+            )
+            for index, (source, target, block) in enumerate(zip(late_in, late_refs, late_blocks))
+        ]
+        for copy in copies:
+            copy.start()
+        waiting = list(copies)
+
+        def wait():
+            while waiting:
+                waiting.pop().wait()
 
         @pl.when(step == 0)
         def _():
@@ -490,7 +508,8 @@
                 [one_row(ref, member) for ref in rows_in],
                 [one_row(ref, member) for ref in rows_out],
                 work,
-                groups[7 + member],
+                groups[8 + member],
+                *([[one_row(ref, member) for ref in late_refs], wait] if late else []),
             )
             for member in range(group)
         )
@@ -507,16 +526,19 @@
         in_specs=[pl.BlockSpec(memory_space=pltpu.SMEM)] * (1 + len(scalars))
         + [by_row(array.shape, group) for array in rowwise]
         + [whole(array.shape) for array in fixed]
-        + [pl.BlockSpec(memory_space=pl.ANY) for array in after],
+        + [pl.BlockSpec(memory_space=pl.ANY) for array in (*after, *late)],
         out_specs=[by_row(part.shape, group) for part in row_outs]
         + [whole(part.shape) for part in sent],
         out_shape=list(row_outs) + list(sent),
-        scratch_shapes=list(shared) + list(private) * group,
+        scratch_shapes=list(shared)
+        + list(private) * group
+        + [vmem(block, part.dtype) for block, part in zip(late_blocks, late)]
+        + ([pltpu.SemaphoreType.DMA((len(late),))] if late else []),
         compiler_params=pltpu.CompilerParams(
             dimension_semantics=("arbitrary",), vmem_limit_bytes=MEMORY
         ),
         cost_estimate=pl.CostEstimate(flops=cost, bytes_accessed=8 * 2**20, transcendentals=0),
-    )(lengths, *scalars, *rowwise, *fixed, *after)
+    )(lengths, *scalars, *rowwise, *fixed, *after, *late)
 
 
 def struct(shape, dtype):
@@ -750,14 +772,14 @@
         set_dense(0, fixed[0], work[16], 3 * width, *work[3:8])
         clear(work[8:15])
 
-    def body(row, lengths_ref, rowwise, outs, work, own):
-        up, low = rowwise[:8], rowwise[8:]
+    def body(row, lengths_ref, up, outs, work, own, low, wait):
         dx_ref = own[0]
         yield from attention_backward(
             row, lengths_ref, up[0][...].astype(LOW), *up[1:7], own[-1], *work[8:10], *own[5:-1]
         )
         dx_ref[...] = up[7][...] + dot_tn(own[-1][...], work[1][...])
         yield
+        wait()
         yield from dense_backward(dx_ref, *low, *work[3:7], *outs, *work[10:15], *own[1:5])
 
     def finish(numbers, work, sent):
@@ -766,14 +788,14 @@
         hand_out(numbers[0], work[15], sent)
 
     return run_rows(
-        body, lengths, list(upper) + list(lower), [urgent] + list(parts),
+        body, lengths, list(upper), [urgent] + list(parts),
         [struct((tokens, width), F32), struct((tokens // SEQ, width, SEQ), LOW)],
         [struct((64, columns), LOW)] * 4,
         attention_weights(width) + dense_weights(width, hidden)
         + attention_sums(width) + dense_sums(width, hidden)
         + [vmem((4, 64, columns), LOW), raw_block(parts)],
         [vmem((SEQ, width), F32)] + dense_work(width, hidden) + BACKWARD_SCRATCH(),
-        15 * 10**9, setup, finish, after, [place], 2,
+        15 * 10**9, setup, finish, after, [place], 2, list(lower),
     )
 
 
@@ -827,7 +849,7 @@
 
     (found,) = run_rows(
         body, lengths, [dqkv, dr], [urgent], [struct((tokens, width), LOW)], [],
-        attention_weights(width), [], 10**10, setup, None, after,
+        attention_weights(width), [], 5 * 10**9, setup, None, after,
     )
     return found
 

time: 166 us -> 166 us (level)
  no operation moved by 1% of the time
where the time goes in v1:
time: 166 us; the launch traced here: 165 us
  Pallas kernels  104 us (63%)
  starting transfers between devices  30.5 us (18%)
  waiting for transfers between devices  25.4 us (15%)
  local copies, waits for them, and re-layouts  3.96 us (2%)
    pallas_call x9, Pallas kernels, run_rows(): pl.pallas_call(kernel, grid=(count // group,), in_specs=[pl.BlockSpec(mem...  92.6 us
    ppermute x24, starting transfers between devices, swap(): lax.ppermute(part, axis, [(source, source ^ step) for source in range(siz...  19 us
    ppermute x24, waiting for transfers between devices, swap(): lax.ppermute(part, axis, [(source, source ^ step) for source in range(siz...  15.8 us
    all_to_all x2, starting transfers between devices, exchange(): return lax.all_to_all(parts, axis, 0, 0, tiled=True)  11.5 us
    all_to_all x2, waiting for transfers between devices, exchange(): return lax.all_to_all(parts, axis, 0, 0, tiled=True)  9.63 us
    pallas_call x3, Pallas kernels, add_parts(): pl.pallas_call(kernel, in_specs=[pl.BlockSpec(memory_space=pltpu.SMEM)] +...  6.28 us
  transfers between devices with their start and end apart: 26, of which 10 were waited for; matrix products, arithmetic and copies ran while one was open for 1% of the time, Pallas kernels for 47%

profile of v1, /device:TPU:0, one launch (start us, length us, event | category | flops | bytes accessed | tf_op | source)
XLA Modules:
  0.0 165.1 jit_solution(10858554411282733814)
XLA Ops:
  0.6 1.8 %shard_map.187 = (bf16[64,3968]{1,0:T(8,128)(2,1)}, bf16[64,2304]{1,0:T(8,128)(2,1)}) custom-call(bf16[2,8,768]{2,1,0:T(8,128)(2,1)} %wq_ref.1, bf16[2,2,8]{2,1,0:T(2,128)(2,1)} %ab_ref.1, bf16[2,8,256]{2,1,0:T(8,128)(2,1)} %wo_ref.1, bf16[2,8,1024]{2,1,0:T(8,128)(2,1)} %wi_ref.1, bf16[2,32]{1,0:T(2,128)(2,1)} %bi_ref.1, bf16[2,32,256]{2,1,0:T(8,128)(2,1)} %wf_ref.1, ...), custom_call_target="tpu_custom_call" | custom-call | tf_op jit(solution)/shard_map/pallas_call | solution.py:905
  2.4 7.3 %all-to-all-start = ((bf16[8,8,3968]{2,1,0:T(8,128)(2,1)}), bf16[8,8,3968]{2,1,0:T(8,128)(2,1)}, u32[]{:S(2)}, u32[]{:S(2)}) async-start(bf16[8,8,3968]{2,1,0:T(8,128)(2,1)} %bitcast.7), calls=%async_computation | async-start | bytes 1015808 | tf_op jit(solution)/shard_map/all_to_all | solution.py:1032
  9.7 4.6 %shard_map.186 = (bf16[2048,256]{1,0:T(8,128)(2,1)}, bf16[2048,256]{1,0:T(8,128)(2,1)}) custom-call(s32[4,6]{1,0:T(4,128)} %lengths_ref.17, bf16[2048,256]{1,0:T(8,128)(2,1)} %refs_0_.1, bf16[2048,256]{1,0:T(8,128)(2,1)} %refs_1_.1), custom_call_target="tpu_custom_call" | custom-call | flops 1000000 | bytes 8388608 | tf_op jit(solution)/shard_map/pallas_call | solution.py:523
  14.3 9.6 %all-to-all-done = bf16[8,8,3968]{2,1,0:T(8,128)(2,1)} async-done(((bf16[8,8,3968]{2,1,0:T(8,128)(2,1)}), bf16[8,8,3968]{2,1,0:T(8,128)(2,1)}, u32[]{:S(2)}, u32[]{:S(2)}) %all-to-all-start) | async-done | bytes 507936 | tf_op jit(solution)/shard_map/all_to_all | solution.py:1032
  24.9 1.6 collective-permute-start.1
  26.8 1.8 %slice.9.refs_4_.refs_3_.refs_10_ = bf16[64,3072]{1,0:T(8,128)(2,1)} slice(bf16[64,3968]{1,0:T(8,128)(2,1)} %shard_map.188), slice={[0:64], [896:3968]} | slice | bytes 786432 | tf_op jit(solution)/shard_map/slice | solution.py:1069
  28.5 1.5 collective-permute-start.4
  30.3 2.6 %collective-permute-done.1.refs_4_ = bf16[64,896]{1,0:T(8,128)(2,1)S(1)} collective-permute-done((bf16[64,896]{1,0:T(8,128)(2,1)S(1)}, bf16[64,896]{1,0:T(8,128)(2,1)S(1)}, u32[]{:S(2)}, u32[]{:S(2)}) %collective-permute-start.1) | collective-permute-done | bytes 114720 | tf_op jit(solution)/shard_map/ppermute | solution.py:1037
  34.2 7.6 %shard_map.189 = (bf16[4,4,128,512]{3,2,1,0:T(8,128)(2,1)}, bf16[4,4,128,512]{3,2,1,0:T(8,128)(2,1)}, bf16[4,4,80,512]{3,2,1,0:T(8,128)(2,1)}, bf16[4,256,512]{2...) custom-call(s32[4,6]{1,0:T(4,128)} %lengths_ref.17, s32[1]{0:T(128)} %bitcast.refs_0_, ...), custom_call_target="tpu_custom_call" | custom-call | flops 4000000000 | bytes 8388608 | tf_op jit(solution)/shard_map/pallas_call | solution.py:523
  41.9 4.3 %all-to-all-start.1 = ((bf16[8,8,2304]{2,1,0:T(8,128)(2,1)}), bf16[8,8,2304]{2,1,0:T(8,128)(2,1)}, u32[]{:S(2)}, u32[]{:S(2)}) async-start(bf16[8,8,2304]{2,1,0:T(8,128)(2,1)} %bitcast.6), calls=%async_computation.1 | async-start | bytes 589824 | tf_op jit(solution)/shard_map/all_to_all | solution.py:1032
  46.2 11.4 %shard_map.191 = (f32[2048,256]{1,0:T(8,128)}, f32[2048,256]{1,0:T(8,128)}, f32[2048,128]{1,0:T(8,128)}, bf16[2048,256]{1,0:T(8,128)(2,1)}, bf16[2048,1024]{1,0:...) custom-call(s32[4,6]{1,0:T(4,128)} %lengths_ref.17, s32[1]{0:T(128)} %bitcast.refs_0_, ...), custom_call_target="tpu_custom_call" | custom-call | flops 5000000000 | bytes 8388608 | tf_op jit(solution)/shard_map/pallas_call | solution.py:523
  57.6 1.1 collective-permute-start.7
  58.7 8.3 %shard_map.192 = (bf16[4,4,128,512]{3,2,1,0:T(8,128)(2,1)}, bf16[4,4,128,512]{3,2,1,0:T(8,128)(2,1)}, bf16[4,4,80,512]{3,2,1,0:T(8,128)(2,1)}, bf16[4,256,512]{2,1,0:T(8,128)(2,1)}, f32[4,8,512]{2,1,0:T(8,128)}) custom-call(s32[4,6]{1,0:T(4,128)} %lengths_ref.17, s32[1]{0:T(128)} %bitcast.refs_0_, f32[2048,256]{1,0:T(8,128)} %get-tuple-element.72.refs_1_, ...), custom_call_target="tpu_custom_call" | custom-call | flops 4000000000 | bytes 8388608 | tf_op jit(solution)/shard_map/pallas_call | solution.py:523
  67.5 1.8 %collective-permute-done.8.refs_8_ = bf16[64,2304]{1,0:T(8,128)(2,1)} collective-permute-done((bf16[64,2304]{1,0:T(8,128)(2,1)}, bf16[64,2304]{1,0:T(8,128)(2,1)}, u32[]{:S(2)}, u32[]{:S(2)}) %collective-permute-start.8) | collective-permute-done | bytes 294944 | tf_op jit(solution)/shard_map/ppermute | solution.py:1037
  69.3 18.9 %shard_map.196 = (bf16[2048,256]{1,0:T(8,128)(2,1)}, f32[2048,256]{1,0:T(8,128)}, bf16[4,256,512]{2,1,0:T(8,128)(2,1)}, bf16[64,2432]{1,0:T(8,128)(2,1)}, bf16[6...) custom-call(s32[4,6]{1,0:T(4,128)} %lengths_ref.17, s32[1]{0:T(128)} %bitcast.refs_0_, ...), custom_call_target="tpu_custom_call" | custom-call | flops 10000000000 | bytes 8388608 | tf_op jit(solution)/shard_map/pallas_call | solution.py:523
  90.2 22.0 %shard_map.197 = (f32[2048,256]{1,0:T(8,128)}, bf16[4,256,512]{2,1,0:T(8,128)(2,1)}, bf16[64,3200]{1,0:T(8,128)(2,1)}, bf16[64,3200]{1,0:T(8,128)(2,1)}, bf16[64...) custom-call(s32[4,6]{1,0:T(4,128)} %lengths_ref.17, s32[1]{0:T(128)} %bitcast.refs_0_, ...), custom_call_target="tpu_custom_call" | custom-call | flops 15000000512 | bytes 8388608 | tf_op jit(solution)/shard_map/pallas_call | solution.py:523
  114.1 2.1 %shard_map.198 = (bf16[32,2432]{1,0:T(8,128)(2,1)}, bf16[32,2432]{1,0:T(8,128)(2,1)}) custom-call(s32[1]{0:T(128)} %bitcast.5.place_ref, bf16[64,2432]{1,0:T(8,128)(2,1)} %get-tuple-element.77.refs_14_.refs_0_, bf16[64,2432]{1,0:T(8,128)(2,1)} %collective-permute-done.9.refs_1_, bf16[64,2432]{1,0:T(8,128)(2,1)} %collective-permute-done.10.refs_2_, ...), custom_call_target="tpu_custom_call" | custom-call | tf_op jit(solution)/shard_map/pallas_call | solution.py:941
  116.3 2.0 %collective-permute-start.12 = (bf16[32,2432]{1,0:T(8,128)(2,1)}, bf16[32,2432]{1,0:T(8,128)(2,1)}, u32[]{:S(2)}, u32[]{:S(2)}) collective-permute-start(bf16[32,2432]{1,0:T(8,128)(2,1)} %get-tuple-element.95), channel_id=1, source_target_pairs={{0,4},{4,0},{8,12},{12,8},{16,20},{20,16},{24,28},{28,24},{1,5},{5... | collective-permute-start | bytes 466952 | tf_op jit(solution)/shard_map/ppermute | solution.py:1037
  118.3 10.5 %shard_map.199 = (bf16[4,768,512]{2,1,0:T(8,128)(2,1)}, bf16[64,896]{1,0:T(8,128)(2,1)}, bf16[64,896]{1,0:T(8,128)(2,1)}, bf16[64,896]{1,0:T(8,128)(2,1)}, bf16[64,896]{1,0:T(8,128)(2,1)}) custom-call(s32[4,6]{1,0:T(4,128)} %lengths_ref.17, s32[1]{0:T(128)} %bitcast.refs_0_, bf16[2048,256]{1,0:T(8,128)(2,1)} %get-tuple-element.68.refs_1_, ...), custom_call_target="tpu_custom_call" | custom-call | flops 8000000000 | bytes 8388608 | tf_op jit(solution)/shard_map/pallas_call | solution.py:523
  130.7 1.9 %collective-permute-done.15.refs_3_ = bf16[64,3200]{1,0:T(8,128)(2,1)} collective-permute-done((bf16[64,3200]{1,0:T(8,128)(2,1)}, bf16[64,3200]{1,0:T(8,128)(2,1)}, u32[]{:S(2)}, u32[]{:S(2)}) %collective-permute-start.15) | collective-permute-done | bytes 409632 | tf_op jit(solution)/shard_map/ppermute | solution.py:1037
  132.6 2.4 %shard_map.200 = (bf16[32,3200]{1,0:T(8,128)(2,1)}, bf16[32,3200]{1,0:T(8,128)(2,1)}) custom-call(s32[1]{0:T(128)} %bitcast.5.place_ref, bf16[64,3200]{1,0:T(8,128)(2,1)} %get-tuple-element.93.refs_4_.refs_8_.refs_0_, bf16[64,3200]{1,0:T(8,128)(2,1)} %collective-permute-done.13.refs_1_, bf16[64,3200]{1,0:T(8,128)(2,1)} %collective-permute-done.14.refs_2_, ...), custom_call_target="tpu_custom_call" | custom-call | tf_op jit(solution)/shard_map/pallas_call | solution.py:941
  135.0 1.6 collective-permute-done.18.refs_2_
  137.2 1.8 %shard_map.201 = (bf16[32,896]{1,0:T(8,128)(2,1)}, bf16[32,896]{1,0:T(8,128)(2,1)}) custom-call(s32[1]{0:T(128)} %bitcast.5.place_ref, bf16[64,896]{1,0:T(8,128)(2,1)} %get-tuple-element.107.refs_0_, bf16[64,896]{1,0:T(8,128)(2,1)} %collective-permute-done.17.refs_1_, bf16[64,896]{1,0:T(8,128)(2,1)} %collective-permute-done.18.refs_2_, ...), custom_call_target="tpu_custom_call" | custom-call | tf_op jit(solution)/shard_map/pallas_call | solution.py:941
  139.0 2.0 %collective-permute-start.20 = (bf16[32,896]{1,0:T(8,128)(2,1)}, bf16[32,896]{1,0:T(8,128)(2,1)}, u32[]{:S(2)}, u32[]{:S(2)}) collective-permute-start(bf16[32,896]{1,0:T(8,128)(2,1)} %get-tuple-element.112), channel_id=1, source_target_pairs={{0,4},{4,0},{8,12},{12,8},{16,20},{20,16},{24,28},{28,24},{1,5},{5... | collective-permute-start | bytes 172040 | tf_op jit(solution)/shard_map/ppermute | solution.py:1037
  141.1 5.4 %shard_map.202.refs_6_ = bf16[2048,256]{1,0:T(8,128)(2,1)} custom-call(s32[4,6]{1,0:T(4,128)} %lengths_ref.17, bf16[4,768,512]{2,1,0:T(8,128)(2,1)} %get-tuple-element.104.refs_5_.refs_0_, f32[2048,256]{1,0:T(8,128)} %get-tuple-element.113.refs_1_, bf16[4,64,896]{2,1,0:T(8,128)(2,1)} %get-tuple-element.71.refs_3_.refs_2_.refs_4_.refs_9_, ...), custom_call_target="tpu_custom_call" | custom-call | flops 5000000000 | bytes 8388608 | tf_op jit(solution)/shard_map/pallas_call | solution.py:523
  146.5 2.3 %collective-permute-done.16.refs_3_ = bf16[32,3200]{1,0:T(8,128)(2,1)} collective-permute-done((bf16[32,3200]{1,0:T(8,128)(2,1)}, bf16[32,3200]{1,0:T(8,128)(2,1)}, u32[]{:S(2)}, u32[]{:S(2)}) %collective-permute-start.16) | collective-permute-done | bytes 204832 | tf_op jit(solution)/shard_map/ppermute | solution.py:1037
  148.8 2.0 %shard_map.203 = (bf16[8,6528]{1,0:T(8,128)(2,1)}, bf16[8,6528]{1,0:T(8,128)(2,1)}, bf16[8,6528]{1,0:T(8,128)(2,1)}, bf16[8,6528]{1,0:T(8,128)(2,1)}) custom-call(s32[1]{0:T(128)} %bitcast.5.place_ref, bf16[32,2432]{1,0:T(8,128)(2,1)} %get-tuple-element.94.refs_9_.refs_0_, bf16[32,2432]{1,0:T(8,128)(2,1)} %collective-permute-done.12.refs_4_.refs_1_, ...), custom_call_target="tpu_custom_call" | custom-call | tf_op jit(solution)/shard_map/pallas_call | solution.py:970
  150.8 1.5 collective-permute-start.21
  152.3 2.4 %collective-permute-start.22 = (bf16[8,6528]{1,0:T(8,128)(2,1)}, bf16[8,6528]{1,0:T(8,128)(2,1)}, u32[]{:S(2)}, u32[]{:S(2)}) collective-permute-start(bf16[8,6528]{1,0:T(8,128)(2,1)} %get-tuple-element.116), channel_id=1, source_target_pairs={{0,16},{4,20},{8,24},{12,28},{16,0},{20,4},{24,8},{28,12},{1,17},{... | collective-permute-start | bytes 313352 | tf_op jit(solution)/shard_map/ppermute | solution.py:1037
  155.2 3.9 %shard_map.204.refs_4_ = bf16[2048,256]{1,0:T(8,128)(2,1)} custom-call(s32[4,6]{1,0:T(4,128)} %lengths_ref.17, bf16[2048,256]{1,0:T(8,128)(2,1)} %get-tuple-element.76.refs_0_, bf16[8,6528]{1,0:T(8,128)(2,1)} %get-tuple-element.114.refs_1_.refs_0_), custom_call_target="tpu_custom_call" | custom-call | flops 3000000000 | bytes 8388608 | tf_op jit(solution)/shard_map/pallas_call | solution.py:523
  159.1 4.3 %collective-permute-done.22.refs_2_ = bf16[8,6528]{1,0:T(8,128)(2,1)} collective-permute-done((bf16[8,6528]{1,0:T(8,128)(2,1)}, bf16[8,6528]{1,0:T(8,128)(2,1)}, u32[]{:S(2)}, u32[]{:S(2)}) %collective-permute-start.22) | collective-permute-done | bytes 104480 | tf_op jit(solution)/shard_map/ppermute | solution.py:1037
  163.4 1.7 %shard_map.205 = (f32[2,8,768]{2,1,0:T(8,128)}, f32[2,2,8]{2,1,0:T(2,128)}, f32[2,8,256]{2,1,0:T(8,128)}, f32[2,8,1024]{2,1,0:T(8,128)}, f32[2,32]{1,0:T(2,128)}...) custom-call(bf16[8,6528]{1,0:T(8,128)(2,1)} %get-tuple-element.114.refs_1_.refs_0_, ...), custom_call_target="tpu_custom_call" | custom-call | tf_op jit(solution)/shard_map/pallas_call | solution.py:1022
  (50 shorter events, 10.5 us)
Async XLA Ops:
  2.4 21.5 %all-to-all-start = ((bf16[8,8,3968]{2,1,0:T(8,128)(2,1)}), bf16[8,8,3968]{2,1,0:T(8,128)(2,1)}, u32[]{:S(2)}, u32[]{:S(2)}) async-start(bf16[8,8,3968]{2,1,0:T(8,128)(2,1)} %bitcast.7), calls=%async_computation | async-start | bytes 1015808 | tf_op jit(solution)/shard_map/all_to_all | solution.py:1032
  24.8 1.7 %copy-start = (bf16[64,896]{1,0:T(8,128)(2,1)}, bf16[64,896]{1,0:T(8,128)(2,1)S(1)}, u32[]{:S(2)}) copy-start(bf16[64,896]{1,0:T(8,128)(2,1)S(1)} %slice.8.refs_2_) | copy-start | bytes 344068
  24.8 5.4 %collective-permute-start.2 = (bf16[64,896]{1,0:T(8,128)(2,1)S(1)}, bf16[64,896]{1,0:T(8,128)(2,1)S(1)}, u32[]{:S(2)}, u32[]{:S(2)}) collective-permute-start(bf16[64,896]{1,0:T(8,128)(2,1)S(1)} %slice.8.refs_2_), channel_id=1, source_target_pairs={{0,3},{1,2},{2,1},{3,0},{4,7},{5,6},{6,5},{7,4},{8,11},{9,10},{10,... | collective-permute-start | bytes 344072 | tf_op jit(solution)/shard_map/ppermute | solution.py:1037
  24.9 8.0 %collective-permute-start.1 = (bf16[64,896]{1,0:T(8,128)(2,1)S(1)}, bf16[64,896]{1,0:T(8,128)(2,1)S(1)}, u32[]{:S(2)}, u32[]{:S(2)}) collective-permute-start(bf16[64,896]{1,0:T(8,128)(2,1)S(1)} %slice.8.refs_2_), channel_id=1, source_target_pairs={{0,2},{1,3},{2,0},{3,1},{4,6},{5,7},{6,4},{7,5},{8,10},{9,11},{10,... | collective-permute-start | bytes 344072 | tf_op jit(solution)/shard_map/ppermute | solution.py:1037
  26.5 6.4 %collective-permute-start = (bf16[64,896]{1,0:T(8,128)(2,1)S(1)}, bf16[64,896]{1,0:T(8,128)(2,1)S(1)}, u32[]{:S(2)}, u32[]{:S(2)}) collective-permute-start(bf16[64,896]{1,0:T(8,128)(2,1)S(1)} %slice.8.refs_2_), channel_id=1, source_target_pairs={{0,1},{1,0},{2,3},{3,2},{4,5},{5,4},{6,7},{7,6},{8,9},{9,8},{10,11... | collective-permute-start | bytes 344072 | tf_op jit(solution)/shard_map/ppermute | solution.py:1037
  28.5 13.2 %collective-permute-start.4 = (bf16[64,3072]{1,0:T(8,128)(2,1)}, bf16[64,3072]{1,0:T(8,128)(2,1)}, u32[]{:S(2)}, u32[]{:S(2)}) collective-permute-start(bf16[64,3072]{1,0:T(8,128)(2,1)} %slice.9.refs_4_.refs_3_.refs_10_), channel_id=1, source_target_pairs={{0,2},{1,3},{2,0},{3,1},{4,6},{5,7},{6,4},{7,5},{8,10},{9,11},{10,... | collective-permute-start | bytes 1179656 | tf_op jit(solution)/shard_map/ppermute | solution.py:1037
  30.1 16.1 %collective-permute-start.3 = (bf16[64,3072]{1,0:T(8,128)(2,1)}, bf16[64,3072]{1,0:T(8,128)(2,1)}, u32[]{:S(2)}, u32[]{:S(2)}) collective-permute-start(bf16[64,3072]{1,0:T(8,128)(2,1)} %slice.9.refs_4_.refs_3_.refs_10_), channel_id=1, source_target_pairs={{0,1},{1,0},{2,3},{3,2},{4,5},{5,4},{6,7},{7,6},{8,9},{9,8},{10,11... | collective-permute-start | bytes 1179656 | tf_op jit(solution)/shard_map/ppermute | solution.py:1037
  30.3 2.6 %copy-start.1 = (bf16[64,896]{1,0:T(8,128)(2,1)}, bf16[64,896]{1,0:T(8,128)(2,1)S(1)}, u32[]{:S(2)}) copy-start(bf16[64,896]{1,0:T(8,128)(2,1)S(1)} %collective-permute-done.2.refs_5_) | copy-start | bytes 344068
  32.9 0.6 copy-start.2
  33.5 0.6 copy-start.3
  41.8 4.4 %collective-permute-start.5 = (bf16[64,3072]{1,0:T(8,128)(2,1)}, bf16[64,3072]{1,0:T(8,128)(2,1)}, u32[]{:S(2)}, u32[]{:S(2)}) collective-permute-start(bf16[64,3072]{1,0:T(8,128)(2,1)} %shard_map.190.refs_6_.refs_5_.refs_12_), channel_id=1, source_target_pairs={{0,1},{1,0},{2,3},{3,2},{4,5},{5,4},{6,7},{7,6},{8,9},{9,8},{10,11... | collective-permute-start | bytes 1179656 | tf_op jit(solution)/shard_map/ppermute | solution.py:1037
  41.9 15.7 %all-to-all-start.1 = ((bf16[8,8,2304]{2,1,0:T(8,128)(2,1)}), bf16[8,8,2304]{2,1,0:T(8,128)(2,1)}, u32[]{:S(2)}, u32[]{:S(2)}) async-start(bf16[8,8,2304]{2,1,0:T(8,128)(2,1)} %bitcast.6), calls=%async_computation.1 | async-start | bytes 589824 | tf_op jit(solution)/shard_map/all_to_all | solution.py:1032
  57.6 9.8 %collective-permute-start.7 = (bf16[64,2304]{1,0:T(8,128)(2,1)}, bf16[64,2304]{1,0:T(8,128)(2,1)}, u32[]{:S(2)}, u32[]{:S(2)}) collective-permute-start(bf16[64,2304]{1,0:T(8,128)(2,1)} %shard_map.194.refs_5_), channel_id=1, source_target_pairs={{0,2},{1,3},{2,0},{3,1},{4,6},{5,7},{6,4},{7,5},{8,10},{9,11},{10,... | collective-permute-start | bytes 884744 | tf_op jit(solution)/shard_map/ppermute | solution.py:1037
  58.7 8.8 %collective-permute-start.6 = (bf16[64,2304]{1,0:T(8,128)(2,1)}, bf16[64,2304]{1,0:T(8,128)(2,1)}, u32[]{:S(2)}, u32[]{:S(2)}) collective-permute-start(bf16[64,2304]{1,0:T(8,128)(2,1)} %shard_map.194.refs_5_), channel_id=1, source_target_pairs={{0,1},{1,0},{2,3},{3,2},{4,5},{5,4},{6,7},{7,6},{8,9},{9,8},{10,11... | collective-permute-start | bytes 884744 | tf_op jit(solution)/shard_map/ppermute | solution.py:1037
  67.3 1.9 %collective-permute-start.8 = (bf16[64,2304]{1,0:T(8,128)(2,1)}, bf16[64,2304]{1,0:T(8,128)(2,1)}, u32[]{:S(2)}, u32[]{:S(2)}) collective-permute-start(bf16[64,2304]{1,0:T(8,128)(2,1)} %shard_map.195.refs_7_), channel_id=1, source_target_pairs={{0,1},{1,0},{2,3},{3,2},{4,5},{5,4},{6,7},{7,6},{8,9},{9,8},{10,11... | collective-permute-start | bytes 884744 | tf_op jit(solution)/shard_map/ppermute | solution.py:1037
  88.2 25.4 %collective-permute-start.9 = (bf16[64,2432]{1,0:T(8,128)(2,1)}, bf16[64,2432]{1,0:T(8,128)(2,1)}, u32[]{:S(2)}, u32[]{:S(2)}) collective-permute-start(bf16[64,2432]{1,0:T(8,128)(2,1)} %get-tuple-element.78), channel_id=1, source_target_pairs={{0,1},{1,0},{2,3},{3,2},{4,5},{5,4},{6,7},{7,6},{8,9},{9,8},{10,11... | collective-permute-start | bytes 933896 | tf_op jit(solution)/shard_map/ppermute | solution.py:1037
  88.5 25.6 %collective-permute-start.10 = (bf16[64,2432]{1,0:T(8,128)(2,1)}, bf16[64,2432]{1,0:T(8,128)(2,1)}, u32[]{:S(2)}, u32[]{:S(2)}) collective-permute-start(bf16[64,2432]{1,0:T(8,128)(2,1)} %get-tuple-element.79), channel_id=1, source_target_pairs={{0,2},{1,3},{2,0},{3,1},{4,6},{5,7},{6,4},{7,5},{8,10},{9,11},{10,... | collective-permute-start | bytes 933896 | tf_op jit(solution)/shard_map/ppermute | solution.py:1037
  89.5 24.7 %collective-permute-start.11 = (bf16[64,2432]{1,0:T(8,128)(2,1)}, bf16[64,2432]{1,0:T(8,128)(2,1)}, u32[]{:S(2)}, u32[]{:S(2)}) collective-permute-start(bf16[64,2432]{1,0:T(8,128)(2,1)} %get-tuple-element.80), channel_id=1, source_target_pairs={{0,3},{1,2},{2,1},{3,0},{4,7},{5,6},{6,5},{7,4},{8,11},{9,10},{10,... | collective-permute-start | bytes 933896 | tf_op jit(solution)/shard_map/ppermute | solution.py:1037
  112.2 17.1 %collective-permute-start.13 = (bf16[64,3200]{1,0:T(8,128)(2,1)}, bf16[64,3200]{1,0:T(8,128)(2,1)}, u32[]{:S(2)}, u32[]{:S(2)}) collective-permute-start(bf16[64,3200]{1,0:T(8,128)(2,1)} %get-tuple-element.96), channel_id=1, source_target_pairs={{0,1},{1,0},{2,3},{3,2},{4,5},{5,4},{6,7},{7,6},{8,9},{9,8},{10,11... | collective-permute-start | bytes 1228808 | tf_op jit(solution)/shard_map/ppermute | solution.py:1037
  112.7 17.3 %collective-permute-start.14 = (bf16[64,3200]{1,0:T(8,128)(2,1)}, bf16[64,3200]{1,0:T(8,128)(2,1)}, u32[]{:S(2)}, u32[]{:S(2)}) collective-permute-start(bf16[64,3200]{1,0:T(8,128)(2,1)} %get-tuple-element.97), channel_id=1, source_target_pairs={{0,2},{1,3},{2,0},{3,1},{4,6},{5,7},{6,4},{7,5},{8,10},{9,11},{10,... | collective-permute-start | bytes 1228808 | tf_op jit(solution)/shard_map/ppermute | solution.py:1037
  113.7 18.9 %collective-permute-start.15 = (bf16[64,3200]{1,0:T(8,128)(2,1)}, bf16[64,3200]{1,0:T(8,128)(2,1)}, u32[]{:S(2)}, u32[]{:S(2)}) collective-permute-start(bf16[64,3200]{1,0:T(8,128)(2,1)} %get-tuple-element.98), channel_id=1, source_target_pairs={{0,3},{1,2},{2,1},{3,0},{4,7},{5,6},{6,5},{7,4},{8,11},{9,10},{10,... | collective-permute-start | bytes 1228808 | tf_op jit(solution)/shard_map/ppermute | solution.py:1037
  116.3 16.3 %collective-permute-start.12 = (bf16[32,2432]{1,0:T(8,128)(2,1)}, bf16[32,2432]{1,0:T(8,128)(2,1)}, u32[]{:S(2)}, u32[]{:S(2)}) collective-permute-start(bf16[32,2432]{1,0:T(8,128)(2,1)} %get-tuple-element.95), channel_id=1, source_target_pairs={{0,4},{4,0},{8,12},{12,8},{16,20},{20,16},{24,28},{28,24},{1,5},{5... | collective-permute-start | bytes 466952 | tf_op jit(solution)/shard_map/ppermute | solution.py:1037
  128.8 6.2 %collective-permute-start.17 = (bf16[64,896]{1,0:T(8,128)(2,1)}, bf16[64,896]{1,0:T(8,128)(2,1)}, u32[]{:S(2)}, u32[]{:S(2)}) collective-permute-start(bf16[64,896]{1,0:T(8,128)(2,1)} %get-tuple-element.108), channel_id=1, source_target_pairs={{0,1},{1,0},{2,3},{3,2},{4,5},{5,4},{6,7},{7,6},{8,9},{9,8},{10,11... | collective-permute-start | bytes 344072 | tf_op jit(solution)/shard_map/ppermute | solution.py:1037
  129.3 7.3 %collective-permute-start.18 = (bf16[64,896]{1,0:T(8,128)(2,1)}, bf16[64,896]{1,0:T(8,128)(2,1)}, u32[]{:S(2)}, u32[]{:S(2)}) collective-permute-start(bf16[64,896]{1,0:T(8,128)(2,1)} %get-tuple-element.109), channel_id=1, source_target_pairs={{0,2},{1,3},{2,0},{3,1},{4,6},{5,7},{6,4},{7,5},{8,10},{9,11},{10,... | collective-permute-start | bytes 344072 | tf_op jit(solution)/shard_map/ppermute | solution.py:1037
  129.9 7.3 %collective-permute-start.19 = (bf16[64,896]{1,0:T(8,128)(2,1)}, bf16[64,896]{1,0:T(8,128)(2,1)}, u32[]{:S(2)}, u32[]{:S(2)}) collective-permute-start(bf16[64,896]{1,0:T(8,128)(2,1)} %get-tuple-element.110), channel_id=1, source_target_pairs={{0,3},{1,2},{2,1},{3,0},{4,7},{5,6},{6,5},{7,4},{8,11},{9,10},{10,... | collective-permute-start | bytes 344072 | tf_op jit(solution)/shard_map/ppermute | solution.py:1037
  139.0 7.5 %collective-permute-start.20 = (bf16[32,896]{1,0:T(8,128)(2,1)}, bf16[32,896]{1,0:T(8,128)(2,1)}, u32[]{:S(2)}, u32[]{:S(2)}) collective-permute-start(bf16[32,896]{1,0:T(8,128)(2,1)} %get-tuple-element.112), channel_id=1, source_target_pairs={{0,4},{4,0},{8,12},{12,8},{16,20},{20,16},{24,28},{28,24},{1,5},{5... | collective-permute-start | bytes 172040 | tf_op jit(solution)/shard_map/ppermute | solution.py:1037
  141.0 7.7 %collective-permute-start.16 = (bf16[32,3200]{1,0:T(8,128)(2,1)}, bf16[32,3200]{1,0:T(8,128)(2,1)}, u32[]{:S(2)}, u32[]{:S(2)}) collective-permute-start(bf16[32,3200]{1,0:T(8,128)(2,1)} %get-tuple-element.106), channel_id=1, source_target_pairs={{0,4},{4,0},{8,12},{12,8},{16,20},{20,16},{24,28},{28,24},{1,5},{5... | collective-permute-start | bytes 614408 | tf_op jit(solution)/shard_map/ppermute | solution.py:1037
  150.8 8.3 %collective-permute-start.21 = (bf16[8,6528]{1,0:T(8,128)(2,1)}, bf16[8,6528]{1,0:T(8,128)(2,1)}, u32[]{:S(2)}, u32[]{:S(2)}) collective-permute-start(bf16[8,6528]{1,0:T(8,128)(2,1)} %get-tuple-element.115), channel_id=1, source_target_pairs={{0,8},{4,12},{8,0},{12,4},{16,24},{20,28},{24,16},{28,20},{1,9},{5... | collective-permute-start | bytes 313352 | tf_op jit(solution)/shard_map/ppermute | solution.py:1037
  152.3 11.0 %collective-permute-start.22 = (bf16[8,6528]{1,0:T(8,128)(2,1)}, bf16[8,6528]{1,0:T(8,128)(2,1)}, u32[]{:S(2)}, u32[]{:S(2)}) collective-permute-start(bf16[8,6528]{1,0:T(8,128)(2,1)} %get-tuple-element.116), channel_id=1, source_target_pairs={{0,16},{4,20},{8,24},{12,28},{16,0},{20,4},{24,8},{28,12},{1,17},{... | collective-permute-start | bytes 313352 | tf_op jit(solution)/shard_map/ppermute | solution.py:1037
  154.7 8.7 %collective-permute-start.23 = (bf16[8,6528]{1,0:T(8,128)(2,1)}, bf16[8,6528]{1,0:T(8,128)(2,1)}, u32[]{:S(2)}, u32[]{:S(2)}) collective-permute-start(bf16[8,6528]{1,0:T(8,128)(2,1)} %get-tuple-element.117), channel_id=1, source_target_pairs={{0,24},{4,28},{8,16},{12,20},{16,8},{20,12},{24,0},{28,4},{1,25},{... | collective-permute-start | bytes 313352 | tf_op jit(solution)/shard_map/ppermute | solution.py:1037

commit v2 on v0

--- a/solution.py
+++ b/solution.py
@@ -463,7 +463,7 @@
 
 def run_rows(
     body, lengths, rowwise, fixed, row_outs, sent, shared, private, cost, setup, finish, after=(),
-    scalars=(), group=1
+    scalars=(), group=1, moved=8
 ):
     count = lengths.shape[0]
     group = group if count % group == 0 else 1
@@ -515,7 +515,9 @@
         compiler_params=pltpu.CompilerParams(
             dimension_semantics=("arbitrary",), vmem_limit_bytes=MEMORY
         ),
-        cost_estimate=pl.CostEstimate(flops=cost, bytes_accessed=8 * 2**20, transcendentals=0),
+        cost_estimate=pl.CostEstimate(
+            flops=cost, bytes_accessed=moved * 2**20, transcendentals=0
+        ),
     )(lengths, *scalars, *rowwise, *fixed, *after)
 
 
@@ -827,7 +829,7 @@
 
     (found,) = run_rows(
         body, lengths, [dqkv, dr], [urgent], [struct((tokens, width), LOW)], [],
-        attention_weights(width), [], 10**10, setup, None, after,
+        attention_weights(width), [], 10**9, setup, None, after, moved=6,
     )
     return found
 

time: 166 us -> 164 us (0.988)
  waiting for transfers between devices: 25.4 us -> 21.8 us
  starting transfers between devices: 30.5 us -> 32.2 us
    ppermute x24, waiting for transfers between devices: 15.8 us -> 12.2 us  [swap(): lax.ppermute(part, axis, [(source, source ^ step) for source in range(siz...]
    ppermute x24, starting transfers between devices: 19 us -> 20.7 us  [swap(): lax.ppermute(part, axis, [(source, source ^ step) for source in range(siz...]
  transfers between devices with their start and end apart: 26 -> 26, of which waited for: 10 -> 8; matrix products, arithmetic and copies ran while one was open for 1% -> 1% of each run, Pallas kernels for 47% -> 49%
where the time goes in v2:
time: 164 us; the launch traced here: 163 us
  Pallas kernels  104 us (63%)
  starting transfers between devices  32.2 us (20%)
  waiting for transfers between devices  21.8 us (13%)
  local copies, waits for them, and re-layouts  3.96 us (2%)
    pallas_call x9, Pallas kernels, run_rows(): pl.pallas_call(kernel, grid=(count // group,), in_specs=[pl.BlockSpec(mem...  92.3 us
    ppermute x24, starting transfers between devices, swap(): lax.ppermute(part, axis, [(source, source ^ step) for source in range(siz...  20.7 us
    ppermute x24, waiting for transfers between devices, swap(): lax.ppermute(part, axis, [(source, source ^ step) for source in range(siz...  12.2 us
    all_to_all x2, starting transfers between devices, exchange(): return lax.all_to_all(parts, axis, 0, 0, tiled=True)  11.5 us
    all_to_all x2, waiting for transfers between devices, exchange(): return lax.all_to_all(parts, axis, 0, 0, tiled=True)  9.63 us
    pallas_call x3, Pallas kernels, add_parts(): pl.pallas_call(kernel, in_specs=[pl.BlockSpec(memory_space=pltpu.SMEM)] +...  6.28 us
  transfers between devices with their start and end apart: 26, of which 8 were waited for; matrix products, arithmetic and copies ran while one was open for 1% of the time, Pallas kernels for 49%

profile of v2, /device:TPU:0, one launch (start us, length us, event | category | flops | bytes accessed | tf_op | source)
XLA Modules:
  0.0 162.9 jit_solution(17946435241955032225)
XLA Ops:
  0.6 1.8 %shard_map.187 = (bf16[64,3968]{1,0:T(8,128)(2,1)}, bf16[64,2304]{1,0:T(8,128)(2,1)}) custom-call(bf16[2,8,768]{2,1,0:T(8,128)(2,1)} %wq_ref.1, bf16[2,2,8]{2,1,0:T(2,128)(2,1)} %ab_ref.1, bf16[2,8,256]{2,1,0:T(8,128)(2,1)} %wo_ref.1, bf16[2,8,1024]{2,1,0:T(8,128)(2,1)} %wi_ref.1, bf16[2,32]{1,0:T(2,128)(2,1)} %bi_ref.1, bf16[2,32,256]{2,1,0:T(8,128)(2,1)} %wf_ref.1, ...), custom_call_target="tpu_custom_call" | custom-call | tf_op jit(solution)/shard_map/pallas_call | solution.py:885
  2.4 7.3 %all-to-all-start = ((bf16[8,8,3968]{2,1,0:T(8,128)(2,1)}), bf16[8,8,3968]{2,1,0:T(8,128)(2,1)}, u32[]{:S(2)}, u32[]{:S(2)}) async-start(bf16[8,8,3968]{2,1,0:T(8,128)(2,1)} %bitcast.7), calls=%async_computation | async-start | bytes 1015808 | tf_op jit(solution)/shard_map/all_to_all | solution.py:1012
  9.7 4.6 %shard_map.186 = (bf16[2048,256]{1,0:T(8,128)(2,1)}, bf16[2048,256]{1,0:T(8,128)(2,1)}) custom-call(s32[4,6]{1,0:T(4,128)} %lengths_ref.17, bf16[2048,256]{1,0:T(8,128)(2,1)} %refs_0_.1, bf16[2048,256]{1,0:T(8,128)(2,1)} %refs_1_.1), custom_call_target="tpu_custom_call" | custom-call | flops 1000000 | bytes 8388608 | tf_op jit(solution)/shard_map/pallas_call | solution.py:504
  14.3 9.6 %all-to-all-done = bf16[8,8,3968]{2,1,0:T(8,128)(2,1)} async-done(((bf16[8,8,3968]{2,1,0:T(8,128)(2,1)}), bf16[8,8,3968]{2,1,0:T(8,128)(2,1)}, u32[]{:S(2)}, u32[]{:S(2)}) %all-to-all-start) | async-done | bytes 507936 | tf_op jit(solution)/shard_map/all_to_all | solution.py:1012
  24.9 1.6 collective-permute-start.1
  26.8 1.8 %slice.9.refs_4_.refs_3_.refs_17_ = bf16[64,3072]{1,0:T(8,128)(2,1)} slice(bf16[64,3968]{1,0:T(8,128)(2,1)} %shard_map.188), slice={[0:64], [896:3968]} | slice | bytes 786432 | tf_op jit(solution)/shard_map/slice | solution.py:1049
  28.5 1.5 collective-permute-start.4
  30.3 2.6 %collective-permute-done.1.refs_4_ = bf16[64,896]{1,0:T(8,128)(2,1)S(1)} collective-permute-done((bf16[64,896]{1,0:T(8,128)(2,1)S(1)}, bf16[64,896]{1,0:T(8,128)(2,1)S(1)}, u32[]{:S(2)}, u32[]{:S(2)}) %collective-permute-start.1) | collective-permute-done | bytes 114720 | tf_op jit(solution)/shard_map/ppermute | solution.py:1017
  34.2 7.6 %shard_map.189 = (bf16[4,4,128,512]{3,2,1,0:T(8,128)(2,1)}, bf16[4,4,128,512]{3,2,1,0:T(8,128)(2,1)}, bf16[4,4,80,512]{3,2,1,0:T(8,128)(2,1)}, bf16[4,256,512]{2...) custom-call(s32[4,6]{1,0:T(4,128)} %lengths_ref.17, s32[1]{0:T(128)} %bitcast.refs_0_, ...), custom_call_target="tpu_custom_call" | custom-call | flops 4000000000 | bytes 8388608 | tf_op jit(solution)/shard_map/pallas_call | solution.py:504
  41.9 4.3 %all-to-all-start.1 = ((bf16[8,8,2304]{2,1,0:T(8,128)(2,1)}), bf16[8,8,2304]{2,1,0:T(8,128)(2,1)}, u32[]{:S(2)}, u32[]{:S(2)}) async-start(bf16[8,8,2304]{2,1,0:T(8,128)(2,1)} %bitcast.6), calls=%async_computation.1 | async-start | bytes 589824 | tf_op jit(solution)/shard_map/all_to_all | solution.py:1012
  46.2 11.4 %shard_map.191 = (f32[2048,256]{1,0:T(8,128)}, f32[2048,256]{1,0:T(8,128)}, f32[2048,128]{1,0:T(8,128)}, bf16[2048,256]{1,0:T(8,128)(2,1)}, bf16[2048,1024]{1,0:...) custom-call(s32[4,6]{1,0:T(4,128)} %lengths_ref.17, s32[1]{0:T(128)} %bitcast.refs_0_, ...), custom_call_target="tpu_custom_call" | custom-call | flops 5000000000 | bytes 8388608 | tf_op jit(solution)/shard_map/pallas_call | solution.py:504
  57.6 1.1 collective-permute-start.7
  58.7 8.3 %shard_map.192 = (bf16[4,4,128,512]{3,2,1,0:T(8,128)(2,1)}, bf16[4,4,128,512]{3,2,1,0:T(8,128)(2,1)}, bf16[4,4,80,512]{3,2,1,0:T(8,128)(2,1)}, bf16[4,256,512]{2,1,0:T(8,128)(2,1)}, f32[4,8,512]{2,1,0:T(8,128)}) custom-call(s32[4,6]{1,0:T(4,128)} %lengths_ref.17, s32[1]{0:T(128)} %bitcast.refs_0_, f32[2048,256]{1,0:T(8,128)} %get-tuple-element.72.refs_1_, ...), custom_call_target="tpu_custom_call" | custom-call | flops 4000000000 | bytes 8388608 | tf_op jit(solution)/shard_map/pallas_call | solution.py:504
  67.5 1.8 %collective-permute-done.8.refs_8_ = bf16[64,2304]{1,0:T(8,128)(2,1)} collective-permute-done((bf16[64,2304]{1,0:T(8,128)(2,1)}, bf16[64,2304]{1,0:T(8,128)(2,1)}, u32[]{:S(2)}, u32[]{:S(2)}) %collective-permute-start.8) | collective-permute-done | bytes 294944 | tf_op jit(solution)/shard_map/ppermute | solution.py:1017
  69.3 18.9 %shard_map.196 = (bf16[2048,256]{1,0:T(8,128)(2,1)}, f32[2048,256]{1,0:T(8,128)}, bf16[4,256,512]{2,1,0:T(8,128)(2,1)}, bf16[64,2432]{1,0:T(8,128)(2,1)}, bf16[6...) custom-call(s32[4,6]{1,0:T(4,128)} %lengths_ref.17, s32[1]{0:T(128)} %bitcast.refs_0_, ...), custom_call_target="tpu_custom_call" | custom-call | flops 10000000000 | bytes 8388608 | tf_op jit(solution)/shard_map/pallas_call | solution.py:504
  88.5 1.0 collective-permute-start.10
  90.2 21.7 %shard_map.197 = (f32[2048,256]{1,0:T(8,128)}, bf16[4,256,512]{2,1,0:T(8,128)(2,1)}, bf16[64,3200]{1,0:T(8,128)(2,1)}, bf16[64,3200]{1,0:T(8,128)(2,1)}, bf16[64...) custom-call(s32[4,6]{1,0:T(4,128)} %lengths_ref.17, s32[1]{0:T(128)} %bitcast.refs_0_, ...), custom_call_target="tpu_custom_call" | custom-call | flops 15000000512 | bytes 8388608 | tf_op jit(solution)/shard_map/pallas_call | solution.py:504
  113.8 2.1 %shard_map.198 = (bf16[32,2432]{1,0:T(8,128)(2,1)}, bf16[32,2432]{1,0:T(8,128)(2,1)}) custom-call(s32[1]{0:T(128)} %bitcast.5.place_ref, bf16[64,2432]{1,0:T(8,128)(2,1)} %get-tuple-element.77.refs_21_.refs_0_, bf16[64,2432]{1,0:T(8,128)(2,1)} %collective-permute-done.9.refs_1_, bf16[64,2432]{1,0:T(8,128)(2,1)} %collective-permute-done.10.refs_2_, ...), custom_call_target="tpu_custom_call" | custom-call | tf_op jit(solution)/shard_map/pallas_call | solution.py:921
  115.9 2.0 %collective-permute-start.12 = (bf16[32,2432]{1,0:T(8,128)(2,1)}, bf16[32,2432]{1,0:T(8,128)(2,1)}, u32[]{:S(2)}, u32[]{:S(2)}) collective-permute-start(bf16[32,2432]{1,0:T(8,128)(2,1)} %get-tuple-element.95), channel_id=1, source_target_pairs={{0,4},{4,0},{8,12},{12,8},{16,20},{20,16},{24,28},{28,24},{1,5},{5... | collective-permute-start | bytes 466952 | tf_op jit(solution)/shard_map/ppermute | solution.py:1017
  118.0 10.5 %shard_map.199 = (bf16[4,768,512]{2,1,0:T(8,128)(2,1)}, bf16[64,896]{1,0:T(8,128)(2,1)}, bf16[64,896]{1,0:T(8,128)(2,1)}, bf16[64,896]{1,0:T(8,128)(2,1)}, bf16[64,896]{1,0:T(8,128)(2,1)}) custom-call(s32[4,6]{1,0:T(4,128)} %lengths_ref.17, s32[1]{0:T(128)} %bitcast.refs_0_, bf16[2048,256]{1,0:T(8,128)(2,1)} %get-tuple-element.68.refs_1_, ...), custom_call_target="tpu_custom_call" | custom-call | flops 8000000000 | bytes 8388608 | tf_op jit(solution)/shard_map/pallas_call | solution.py:504
  130.4 1.9 %collective-permute-done.15.refs_3_ = bf16[64,3200]{1,0:T(8,128)(2,1)} collective-permute-done((bf16[64,3200]{1,0:T(8,128)(2,1)}, bf16[64,3200]{1,0:T(8,128)(2,1)}, u32[]{:S(2)}, u32[]{:S(2)}) %collective-permute-start.15) | collective-permute-done | bytes 409632 | tf_op jit(solution)/shard_map/ppermute | solution.py:1017
  132.3 2.4 %shard_map.200 = (bf16[32,3200]{1,0:T(8,128)(2,1)}, bf16[32,3200]{1,0:T(8,128)(2,1)}) custom-call(s32[1]{0:T(128)} %bitcast.5.place_ref, bf16[64,3200]{1,0:T(8,128)(2,1)} %get-tuple-element.93.refs_4_.refs_8_.refs_0_, bf16[64,3200]{1,0:T(8,128)(2,1)} %collective-permute-done.13.refs_1_, bf16[64,3200]{1,0:T(8,128)(2,1)} %collective-permute-done.14.refs_2_, ...), custom_call_target="tpu_custom_call" | custom-call | tf_op jit(solution)/shard_map/pallas_call | solution.py:921
  134.7 1.7 %collective-permute-start.16 = (bf16[32,3200]{1,0:T(8,128)(2,1)}, bf16[32,3200]{1,0:T(8,128)(2,1)}, u32[]{:S(2)}, u32[]{:S(2)}) collective-permute-start(bf16[32,3200]{1,0:T(8,128)(2,1)} %get-tuple-element.106), channel_id=1, source_target_pairs={{0,4},{4,0},{8,12},{12,8},{16,20},{20,16},{24,28},{28,24},{1,5},{5... | collective-permute-start | bytes 614408 | tf_op jit(solution)/shard_map/ppermute | solution.py:1017
  136.9 1.8 %shard_map.201 = (bf16[32,896]{1,0:T(8,128)(2,1)}, bf16[32,896]{1,0:T(8,128)(2,1)}) custom-call(s32[1]{0:T(128)} %bitcast.5.place_ref, bf16[64,896]{1,0:T(8,128)(2,1)} %get-tuple-element.107.refs_0_, bf16[64,896]{1,0:T(8,128)(2,1)} %collective-permute-done.17.refs_1_, bf16[64,896]{1,0:T(8,128)(2,1)} %collective-permute-done.18.refs_2_, ...), custom_call_target="tpu_custom_call" | custom-call | tf_op jit(solution)/shard_map/pallas_call | solution.py:921
  138.7 2.0 %collective-permute-start.20 = (bf16[32,896]{1,0:T(8,128)(2,1)}, bf16[32,896]{1,0:T(8,128)(2,1)}, u32[]{:S(2)}, u32[]{:S(2)}) collective-permute-start(bf16[32,896]{1,0:T(8,128)(2,1)} %get-tuple-element.112), channel_id=1, source_target_pairs={{0,4},{4,0},{8,12},{12,8},{16,20},{20,16},{24,28},{28,24},{1,5},{5... | collective-permute-start | bytes 172040 | tf_op jit(solution)/shard_map/ppermute | solution.py:1017
  140.7 5.4 %shard_map.202.refs_6_ = bf16[2048,256]{1,0:T(8,128)(2,1)} custom-call(s32[4,6]{1,0:T(4,128)} %lengths_ref.17, bf16[4,768,512]{2,1,0:T(8,128)(2,1)} %get-tuple-element.104.refs_5_.refs_0_, f32[2048,256]{1,0:T(8,128)} %get-tuple-element.113.refs_1_, bf16[4,64,896]{2,1,0:T(8,128)(2,1)} %get-tuple-element.71.refs_3_.refs_2_.refs_4_.refs_16_, ...), custom_call_target="tpu_custom_call" | custom-call | flops 1000000000 | bytes 6291456 | tf_op jit(solution)/shard_map/pallas_call | solution.py:504
  146.2 2.0 %shard_map.203 = (bf16[8,6528]{1,0:T(8,128)(2,1)}, bf16[8,6528]{1,0:T(8,128)(2,1)}, bf16[8,6528]{1,0:T(8,128)(2,1)}, bf16[8,6528]{1,0:T(8,128)(2,1)}) custom-call(s32[1]{0:T(128)} %bitcast.5.place_ref, bf16[32,2432]{1,0:T(8,128)(2,1)} %get-tuple-element.94.refs_9_.refs_0_, bf16[32,2432]{1,0:T(8,128)(2,1)} %collective-permute-done.12.refs_4_.refs_1_, ...), custom_call_target="tpu_custom_call" | custom-call | tf_op jit(solution)/shard_map/pallas_call | solution.py:950
  148.2 1.5 collective-permute-start.21
  149.7 2.4 %collective-permute-start.22 = (bf16[8,6528]{1,0:T(8,128)(2,1)}, bf16[8,6528]{1,0:T(8,128)(2,1)}, u32[]{:S(2)}, u32[]{:S(2)}) collective-permute-start(bf16[8,6528]{1,0:T(8,128)(2,1)} %get-tuple-element.116), channel_id=1, source_target_pairs={{0,16},{4,20},{8,24},{12,28},{16,0},{20,4},{24,8},{28,12},{1,17},{... | collective-permute-start | bytes 313352 | tf_op jit(solution)/shard_map/ppermute | solution.py:1017
  152.6 3.9 %shard_map.204.refs_4_ = bf16[2048,256]{1,0:T(8,128)(2,1)} custom-call(s32[4,6]{1,0:T(4,128)} %lengths_ref.17, bf16[2048,256]{1,0:T(8,128)(2,1)} %get-tuple-element.76.refs_0_, bf16[8,6528]{1,0:T(8,128)(2,1)} %get-tuple-element.114.refs_1_.refs_0_), custom_call_target="tpu_custom_call" | custom-call | flops 3000000000 | bytes 8388608 | tf_op jit(solution)/shard_map/pallas_call | solution.py:504
  156.5 4.7 %collective-permute-done.22.refs_2_ = bf16[8,6528]{1,0:T(8,128)(2,1)} collective-permute-done((bf16[8,6528]{1,0:T(8,128)(2,1)}, bf16[8,6528]{1,0:T(8,128)(2,1)}, u32[]{:S(2)}, u32[]{:S(2)}) %collective-permute-start.22) | collective-permute-done | bytes 104480 | tf_op jit(solution)/shard_map/ppermute | solution.py:1017
  161.2 1.7 %shard_map.205 = (f32[2,8,768]{2,1,0:T(8,128)}, f32[2,2,8]{2,1,0:T(2,128)}, f32[2,8,256]{2,1,0:T(8,128)}, f32[2,8,1024]{2,1,0:T(8,128)}, f32[2,32]{1,0:T(2,128)}...) custom-call(bf16[8,6528]{1,0:T(8,128)(2,1)} %get-tuple-element.114.refs_1_.refs_0_, ...), custom_call_target="tpu_custom_call" | custom-call | tf_op jit(solution)/shard_map/pallas_call | solution.py:1002
  (50 shorter events, 9.3 us)
Async XLA Ops:
  2.4 21.5 %all-to-all-start = ((bf16[8,8,3968]{2,1,0:T(8,128)(2,1)}), bf16[8,8,3968]{2,1,0:T(8,128)(2,1)}, u32[]{:S(2)}, u32[]{:S(2)}) async-start(bf16[8,8,3968]{2,1,0:T(8,128)(2,1)} %bitcast.7), calls=%async_computation | async-start | bytes 1015808 | tf_op jit(solution)/shard_map/all_to_all | solution.py:1012
  24.8 1.7 %copy-start = (bf16[64,896]{1,0:T(8,128)(2,1)}, bf16[64,896]{1,0:T(8,128)(2,1)S(1)}, u32[]{:S(2)}) copy-start(bf16[64,896]{1,0:T(8,128)(2,1)S(1)} %slice.8.refs_2_) | copy-start | bytes 344068
  24.8 5.4 %collective-permute-start.2 = (bf16[64,896]{1,0:T(8,128)(2,1)S(1)}, bf16[64,896]{1,0:T(8,128)(2,1)S(1)}, u32[]{:S(2)}, u32[]{:S(2)}) collective-permute-start(bf16[64,896]{1,0:T(8,128)(2,1)S(1)} %slice.8.refs_2_), channel_id=1, source_target_pairs={{0,3},{1,2},{2,1},{3,0},{4,7},{5,6},{6,5},{7,4},{8,11},{9,10},{10,... | collective-permute-start | bytes 344072 | tf_op jit(solution)/shard_map/ppermute | solution.py:1017
  24.9 8.0 %collective-permute-start.1 = (bf16[64,896]{1,0:T(8,128)(2,1)S(1)}, bf16[64,896]{1,0:T(8,128)(2,1)S(1)}, u32[]{:S(2)}, u32[]{:S(2)}) collective-permute-start(bf16[64,896]{1,0:T(8,128)(2,1)S(1)} %slice.8.refs_2_), channel_id=1, source_target_pairs={{0,2},{1,3},{2,0},{3,1},{4,6},{5,7},{6,4},{7,5},{8,10},{9,11},{10,... | collective-permute-start | bytes 344072 | tf_op jit(solution)/shard_map/ppermute | solution.py:1017
  26.5 6.4 %collective-permute-start = (bf16[64,896]{1,0:T(8,128)(2,1)S(1)}, bf16[64,896]{1,0:T(8,128)(2,1)S(1)}, u32[]{:S(2)}, u32[]{:S(2)}) collective-permute-start(bf16[64,896]{1,0:T(8,128)(2,1)S(1)} %slice.8.refs_2_), channel_id=1, source_target_pairs={{0,1},{1,0},{2,3},{3,2},{4,5},{5,4},{6,7},{7,6},{8,9},{9,8},{10,11... | collective-permute-start | bytes 344072 | tf_op jit(solution)/shard_map/ppermute | solution.py:1017
  28.5 13.2 %collective-permute-start.4 = (bf16[64,3072]{1,0:T(8,128)(2,1)}, bf16[64,3072]{1,0:T(8,128)(2,1)}, u32[]{:S(2)}, u32[]{:S(2)}) collective-permute-start(bf16[64,3072]{1,0:T(8,128)(2,1)} %slice.9.refs_4_.refs_3_.refs_17_), channel_id=1, source_target_pairs={{0,2},{1,3},{2,0},{3,1},{4,6},{5,7},{6,4},{7,5},{8,10},{9,11},{10,... | collective-permute-start | bytes 1179656 | tf_op jit(solution)/shard_map/ppermute | solution.py:1017
  30.1 16.1 %collective-permute-start.3 = (bf16[64,3072]{1,0:T(8,128)(2,1)}, bf16[64,3072]{1,0:T(8,128)(2,1)}, u32[]{:S(2)}, u32[]{:S(2)}) collective-permute-start(bf16[64,3072]{1,0:T(8,128)(2,1)} %slice.9.refs_4_.refs_3_.refs_17_), channel_id=1, source_target_pairs={{0,1},{1,0},{2,3},{3,2},{4,5},{5,4},{6,7},{7,6},{8,9},{9,8},{10,11... | collective-permute-start | bytes 1179656 | tf_op jit(solution)/shard_map/ppermute | solution.py:1017
  30.3 2.6 %copy-start.1 = (bf16[64,896]{1,0:T(8,128)(2,1)}, bf16[64,896]{1,0:T(8,128)(2,1)S(1)}, u32[]{:S(2)}) copy-start(bf16[64,896]{1,0:T(8,128)(2,1)S(1)} %collective-permute-done.2.refs_5_) | copy-start | bytes 344068
  32.9 0.6 copy-start.2
  33.5 0.6 copy-start.3
  41.8 4.4 %collective-permute-start.5 = (bf16[64,3072]{1,0:T(8,128)(2,1)}, bf16[64,3072]{1,0:T(8,128)(2,1)}, u32[]{:S(2)}, u32[]{:S(2)}) collective-permute-start(bf16[64,3072]{1,0:T(8,128)(2,1)} %shard_map.190.refs_6_.refs_5_.refs_19_), channel_id=1, source_target_pairs={{0,1},{1,0},{2,3},{3,2},{4,5},{5,4},{6,7},{7,6},{8,9},{9,8},{10,11... | collective-permute-start | bytes 1179656 | tf_op jit(solution)/shard_map/ppermute | solution.py:1017
  41.9 15.7 %all-to-all-start.1 = ((bf16[8,8,2304]{2,1,0:T(8,128)(2,1)}), bf16[8,8,2304]{2,1,0:T(8,128)(2,1)}, u32[]{:S(2)}, u32[]{:S(2)}) async-start(bf16[8,8,2304]{2,1,0:T(8,128)(2,1)} %bitcast.6), calls=%async_computation.1 | async-start | bytes 589824 | tf_op jit(solution)/shard_map/all_to_all | solution.py:1012
  57.6 9.8 %collective-permute-start.7 = (bf16[64,2304]{1,0:T(8,128)(2,1)}, bf16[64,2304]{1,0:T(8,128)(2,1)}, u32[]{:S(2)}, u32[]{:S(2)}) collective-permute-start(bf16[64,2304]{1,0:T(8,128)(2,1)} %shard_map.194.refs_5_), channel_id=1, source_target_pairs={{0,2},{1,3},{2,0},{3,1},{4,6},{5,7},{6,4},{7,5},{8,10},{9,11},{10,... | collective-permute-start | bytes 884744 | tf_op jit(solution)/shard_map/ppermute | solution.py:1017
  58.7 8.8 %collective-permute-start.6 = (bf16[64,2304]{1,0:T(8,128)(2,1)}, bf16[64,2304]{1,0:T(8,128)(2,1)}, u32[]{:S(2)}, u32[]{:S(2)}) collective-permute-start(bf16[64,2304]{1,0:T(8,128)(2,1)} %shard_map.194.refs_5_), channel_id=1, source_target_pairs={{0,1},{1,0},{2,3},{3,2},{4,5},{5,4},{6,7},{7,6},{8,9},{9,8},{10,11... | collective-permute-start | bytes 884744 | tf_op jit(solution)/shard_map/ppermute | solution.py:1017
  67.3 1.9 %collective-permute-start.8 = (bf16[64,2304]{1,0:T(8,128)(2,1)}, bf16[64,2304]{1,0:T(8,128)(2,1)}, u32[]{:S(2)}, u32[]{:S(2)}) collective-permute-start(bf16[64,2304]{1,0:T(8,128)(2,1)} %shard_map.195.refs_7_), channel_id=1, source_target_pairs={{0,1},{1,0},{2,3},{3,2},{4,5},{5,4},{6,7},{7,6},{8,9},{9,8},{10,11... | collective-permute-start | bytes 884744 | tf_op jit(solution)/shard_map/ppermute | solution.py:1017
  88.2 25.1 %collective-permute-start.9 = (bf16[64,2432]{1,0:T(8,128)(2,1)}, bf16[64,2432]{1,0:T(8,128)(2,1)}, u32[]{:S(2)}, u32[]{:S(2)}) collective-permute-start(bf16[64,2432]{1,0:T(8,128)(2,1)} %get-tuple-element.78), channel_id=1, source_target_pairs={{0,1},{1,0},{2,3},{3,2},{4,5},{5,4},{6,7},{7,6},{8,9},{9,8},{10,11... | collective-permute-start | bytes 933896 | tf_op jit(solution)/shard_map/ppermute | solution.py:1017
  88.5 25.3 %collective-permute-start.10 = (bf16[64,2432]{1,0:T(8,128)(2,1)}, bf16[64,2432]{1,0:T(8,128)(2,1)}, u32[]{:S(2)}, u32[]{:S(2)}) collective-permute-start(bf16[64,2432]{1,0:T(8,128)(2,1)} %get-tuple-element.79), channel_id=1, source_target_pairs={{0,2},{1,3},{2,0},{3,1},{4,6},{5,7},{6,4},{7,5},{8,10},{9,11},{10,... | collective-permute-start | bytes 933896 | tf_op jit(solution)/shard_map/ppermute | solution.py:1017
  89.5 24.3 %collective-permute-start.11 = (bf16[64,2432]{1,0:T(8,128)(2,1)}, bf16[64,2432]{1,0:T(8,128)(2,1)}, u32[]{:S(2)}, u32[]{:S(2)}) collective-permute-start(bf16[64,2432]{1,0:T(8,128)(2,1)} %get-tuple-element.80), channel_id=1, source_target_pairs={{0,3},{1,2},{2,1},{3,0},{4,7},{5,6},{6,5},{7,4},{8,11},{9,10},{10,... | collective-permute-start | bytes 933896 | tf_op jit(solution)/shard_map/ppermute | solution.py:1017
  111.9 17.1 %collective-permute-start.13 = (bf16[64,3200]{1,0:T(8,128)(2,1)}, bf16[64,3200]{1,0:T(8,128)(2,1)}, u32[]{:S(2)}, u32[]{:S(2)}) collective-permute-start(bf16[64,3200]{1,0:T(8,128)(2,1)} %get-tuple-element.96), channel_id=1, source_target_pairs={{0,1},{1,0},{2,3},{3,2},{4,5},{5,4},{6,7},{7,6},{8,9},{9,8},{10,11... | collective-permute-start | bytes 1228808 | tf_op jit(solution)/shard_map/ppermute | solution.py:1017
  112.4 17.3 %collective-permute-start.14 = (bf16[64,3200]{1,0:T(8,128)(2,1)}, bf16[64,3200]{1,0:T(8,128)(2,1)}, u32[]{:S(2)}, u32[]{:S(2)}) collective-permute-start(bf16[64,3200]{1,0:T(8,128)(2,1)} %get-tuple-element.97), channel_id=1, source_target_pairs={{0,2},{1,3},{2,0},{3,1},{4,6},{5,7},{6,4},{7,5},{8,10},{9,11},{10,... | collective-permute-start | bytes 1228808 | tf_op jit(solution)/shard_map/ppermute | solution.py:1017
  113.4 18.9 %collective-permute-start.15 = (bf16[64,3200]{1,0:T(8,128)(2,1)}, bf16[64,3200]{1,0:T(8,128)(2,1)}, u32[]{:S(2)}, u32[]{:S(2)}) collective-permute-start(bf16[64,3200]{1,0:T(8,128)(2,1)} %get-tuple-element.98), channel_id=1, source_target_pairs={{0,3},{1,2},{2,1},{3,0},{4,7},{5,6},{6,5},{7,4},{8,11},{9,10},{10,... | collective-permute-start | bytes 1228808 | tf_op jit(solution)/shard_map/ppermute | solution.py:1017
  115.9 16.3 %collective-permute-start.12 = (bf16[32,2432]{1,0:T(8,128)(2,1)}, bf16[32,2432]{1,0:T(8,128)(2,1)}, u32[]{:S(2)}, u32[]{:S(2)}) collective-permute-start(bf16[32,2432]{1,0:T(8,128)(2,1)} %get-tuple-element.95), channel_id=1, source_target_pairs={{0,4},{4,0},{8,12},{12,8},{16,20},{20,16},{24,28},{28,24},{1,5},{5... | collective-permute-start | bytes 466952 | tf_op jit(solution)/shard_map/ppermute | solution.py:1017
  128.4 8.0 %collective-permute-start.17 = (bf16[64,896]{1,0:T(8,128)(2,1)}, bf16[64,896]{1,0:T(8,128)(2,1)}, u32[]{:S(2)}, u32[]{:S(2)}) collective-permute-start(bf16[64,896]{1,0:T(8,128)(2,1)} %get-tuple-element.108), channel_id=1, source_target_pairs={{0,1},{1,0},{2,3},{3,2},{4,5},{5,4},{6,7},{7,6},{8,9},{9,8},{10,11... | collective-permute-start | bytes 344072 | tf_op jit(solution)/shard_map/ppermute | solution.py:1017
  128.9 7.5 %collective-permute-start.18 = (bf16[64,896]{1,0:T(8,128)(2,1)}, bf16[64,896]{1,0:T(8,128)(2,1)}, u32[]{:S(2)}, u32[]{:S(2)}) collective-permute-start(bf16[64,896]{1,0:T(8,128)(2,1)} %get-tuple-element.109), channel_id=1, source_target_pairs={{0,2},{1,3},{2,0},{3,1},{4,6},{5,7},{6,4},{7,5},{8,10},{9,11},{10,... | collective-permute-start | bytes 344072 | tf_op jit(solution)/shard_map/ppermute | solution.py:1017
  129.6 7.3 %collective-permute-start.19 = (bf16[64,896]{1,0:T(8,128)(2,1)}, bf16[64,896]{1,0:T(8,128)(2,1)}, u32[]{:S(2)}, u32[]{:S(2)}) collective-permute-start(bf16[64,896]{1,0:T(8,128)(2,1)} %get-tuple-element.110), channel_id=1, source_target_pairs={{0,3},{1,2},{2,1},{3,0},{4,7},{5,6},{6,5},{7,4},{8,11},{9,10},{10,... | collective-permute-start | bytes 344072 | tf_op jit(solution)/shard_map/ppermute | solution.py:1017
  134.7 11.5 %collective-permute-start.16 = (bf16[32,3200]{1,0:T(8,128)(2,1)}, bf16[32,3200]{1,0:T(8,128)(2,1)}, u32[]{:S(2)}, u32[]{:S(2)}) collective-permute-start(bf16[32,3200]{1,0:T(8,128)(2,1)} %get-tuple-element.106), channel_id=1, source_target_pairs={{0,4},{4,0},{8,12},{12,8},{16,20},{20,16},{24,28},{28,24},{1,5},{5... | collective-permute-start | bytes 614408 | tf_op jit(solution)/shard_map/ppermute | solution.py:1017
  138.7 7.4 %collective-permute-start.20 = (bf16[32,896]{1,0:T(8,128)(2,1)}, bf16[32,896]{1,0:T(8,128)(2,1)}, u32[]{:S(2)}, u32[]{:S(2)}) collective-permute-start(bf16[32,896]{1,0:T(8,128)(2,1)} %get-tuple-element.112), channel_id=1, source_target_pairs={{0,4},{4,0},{8,12},{12,8},{16,20},{20,16},{24,28},{28,24},{1,5},{5... | collective-permute-start | bytes 172040 | tf_op jit(solution)/shard_map/ppermute | solution.py:1017
  148.2 8.3 %collective-permute-start.21 = (bf16[8,6528]{1,0:T(8,128)(2,1)}, bf16[8,6528]{1,0:T(8,128)(2,1)}, u32[]{:S(2)}, u32[]{:S(2)}) collective-permute-start(bf16[8,6528]{1,0:T(8,128)(2,1)} %get-tuple-element.115), channel_id=1, source_target_pairs={{0,8},{4,12},{8,0},{12,4},{16,24},{20,28},{24,16},{28,20},{1,9},{5... | collective-permute-start | bytes 313352 | tf_op jit(solution)/shard_map/ppermute | solution.py:1017
  149.7 11.5 %collective-permute-start.22 = (bf16[8,6528]{1,0:T(8,128)(2,1)}, bf16[8,6528]{1,0:T(8,128)(2,1)}, u32[]{:S(2)}, u32[]{:S(2)}) collective-permute-start(bf16[8,6528]{1,0:T(8,128)(2,1)} %get-tuple-element.116), channel_id=1, source_target_pairs={{0,16},{4,20},{8,24},{12,28},{16,0},{20,4},{24,8},{28,12},{1,17},{... | collective-permute-start | bytes 313352 | tf_op jit(solution)/shard_map/ppermute | solution.py:1017
  152.0 9.1 %collective-permute-start.23 = (bf16[8,6528]{1,0:T(8,128)(2,1)}, bf16[8,6528]{1,0:T(8,128)(2,1)}, u32[]{:S(2)}, u32[]{:S(2)}) collective-permute-start(bf16[8,6528]{1,0:T(8,128)(2,1)} %get-tuple-element.117), channel_id=1, source_target_pairs={{0,24},{4,28},{8,16},{12,20},{16,8},{20,12},{24,0},{28,4},{1,25},{... | collective-permute-start | bytes 313352 | tf_op jit(solution)/shard_map/ppermute | solution.py:1017

commit v3 on v2

--- a/solution.py
+++ b/solution.py
@@ -18,7 +18,7 @@
 FLOOR = -1e20
 EPSILON = 1e-12
 PIECE = 256
-SMALL = 128
+SMALL = 64
 GROUPS = (4, 8, 8)
 DEVICES = 32
 LOW = jnp.bfloat16

time: 164 us -> 164 us (level)
  no operation moved by 1% of the time
where the time goes in v3:
time: 164 us; the launch traced here: 163 us
  Pallas kernels  104 us (63%)
  starting transfers between devices  32.2 us (20%)
  waiting for transfers between devices  21.8 us (13%)
  local copies, waits for them, and re-layouts  3.96 us (2%)
    pallas_call x9, Pallas kernels, run_rows(): pl.pallas_call(kernel, grid=(count // group,), in_specs=[pl.BlockSpec(mem...  92.3 us
    ppermute x24, starting transfers between devices, swap(): lax.ppermute(part, axis, [(source, source ^ step) for source in range(siz...  20.7 us
    ppermute x24, waiting for transfers between devices, swap(): lax.ppermute(part, axis, [(source, source ^ step) for source in range(siz...  12.2 us
    all_to_all x2, starting transfers between devices, exchange(): return lax.all_to_all(parts, axis, 0, 0, tiled=True)  11.5 us
    all_to_all x2, waiting for transfers between devices, exchange(): return lax.all_to_all(parts, axis, 0, 0, tiled=True)  9.63 us
    pallas_call x3, Pallas kernels, add_parts(): pl.pallas_call(kernel, in_specs=[pl.BlockSpec(memory_space=pltpu.SMEM)] +...  6.28 us
  transfers between devices with their start and end apart: 26, of which 8 were waited for; matrix products, arithmetic and copies ran while one was open for 1% of the time, Pallas kernels for 49%

profile of v3, /device:TPU:0, one launch (start us, length us, event | category | flops | bytes accessed | tf_op | source)
XLA Modules:
  0.0 162.9 jit_solution(6888892391479856273)
XLA Ops:
  0.6 1.8 %shard_map.187 = (bf16[64,3968]{1,0:T(8,128)(2,1)}, bf16[64,2304]{1,0:T(8,128)(2,1)}) custom-call(bf16[2,8,768]{2,1,0:T(8,128)(2,1)} %wq_ref.1, bf16[2,2,8]{2,1,0:T(2,128)(2,1)} %ab_ref.1, bf16[2,8,256]{2,1,0:T(8,128)(2,1)} %wo_ref.1, bf16[2,8,1024]{2,1,0:T(8,128)(2,1)} %wi_ref.1, bf16[2,32]{1,0:T(2,128)(2,1)} %bi_ref.1, bf16[2,32,256]{2,1,0:T(8,128)(2,1)} %wf_ref.1, ...), custom_call_target="tpu_custom_call" | custom-call | tf_op jit(solution)/shard_map/pallas_call | solution.py:885
  2.4 7.3 %all-to-all-start = ((bf16[8,8,3968]{2,1,0:T(8,128)(2,1)}), bf16[8,8,3968]{2,1,0:T(8,128)(2,1)}, u32[]{:S(2)}, u32[]{:S(2)}) async-start(bf16[8,8,3968]{2,1,0:T(8,128)(2,1)} %bitcast.7), calls=%async_computation | async-start | bytes 1015808 | tf_op jit(solution)/shard_map/all_to_all | solution.py:1012
  9.7 4.6 %shard_map.186 = (bf16[2048,256]{1,0:T(8,128)(2,1)}, bf16[2048,256]{1,0:T(8,128)(2,1)}) custom-call(s32[4,6]{1,0:T(4,128)} %lengths_ref.17, bf16[2048,256]{1,0:T(8,128)(2,1)} %refs_0_.1, bf16[2048,256]{1,0:T(8,128)(2,1)} %refs_1_.1), custom_call_target="tpu_custom_call" | custom-call | flops 1000000 | bytes 8388608 | tf_op jit(solution)/shard_map/pallas_call | solution.py:504
  14.3 9.6 %all-to-all-done = bf16[8,8,3968]{2,1,0:T(8,128)(2,1)} async-done(((bf16[8,8,3968]{2,1,0:T(8,128)(2,1)}), bf16[8,8,3968]{2,1,0:T(8,128)(2,1)}, u32[]{:S(2)}, u32[]{:S(2)}) %all-to-all-start) | async-done | bytes 507936 | tf_op jit(solution)/shard_map/all_to_all | solution.py:1012
  24.9 1.6 collective-permute-start.1
  26.8 1.8 %slice.9.refs_4_.refs_3_.refs_17_ = bf16[64,3072]{1,0:T(8,128)(2,1)} slice(bf16[64,3968]{1,0:T(8,128)(2,1)} %shard_map.188), slice={[0:64], [896:3968]} | slice | bytes 786432 | tf_op jit(solution)/shard_map/slice | solution.py:1049
  28.5 1.5 collective-permute-start.4
  30.3 2.6 %collective-permute-done.1.refs_4_ = bf16[64,896]{1,0:T(8,128)(2,1)S(1)} collective-permute-done((bf16[64,896]{1,0:T(8,128)(2,1)S(1)}, bf16[64,896]{1,0:T(8,128)(2,1)S(1)}, u32[]{:S(2)}, u32[]{:S(2)}) %collective-permute-start.1) | collective-permute-done | bytes 114720 | tf_op jit(solution)/shard_map/ppermute | solution.py:1017
  34.2 7.6 %shard_map.189 = (bf16[4,4,128,512]{3,2,1,0:T(8,128)(2,1)}, bf16[4,4,128,512]{3,2,1,0:T(8,128)(2,1)}, bf16[4,4,80,512]{3,2,1,0:T(8,128)(2,1)}, bf16[4,256,512]{2...) custom-call(s32[4,6]{1,0:T(4,128)} %lengths_ref.17, s32[1]{0:T(128)} %bitcast.refs_0_, ...), custom_call_target="tpu_custom_call" | custom-call | flops 4000000000 | bytes 8388608 | tf_op jit(solution)/shard_map/pallas_call | solution.py:504
  41.9 4.3 %all-to-all-start.1 = ((bf16[8,8,2304]{2,1,0:T(8,128)(2,1)}), bf16[8,8,2304]{2,1,0:T(8,128)(2,1)}, u32[]{:S(2)}, u32[]{:S(2)}) async-start(bf16[8,8,2304]{2,1,0:T(8,128)(2,1)} %bitcast.6), calls=%async_computation.1 | async-start | bytes 589824 | tf_op jit(solution)/shard_map/all_to_all | solution.py:1012
  46.2 11.4 %shard_map.191 = (f32[2048,256]{1,0:T(8,128)}, f32[2048,256]{1,0:T(8,128)}, f32[2048,128]{1,0:T(8,128)}, bf16[2048,256]{1,0:T(8,128)(2,1)}, bf16[2048,1024]{1,0:...) custom-call(s32[4,6]{1,0:T(4,128)} %lengths_ref.17, s32[1]{0:T(128)} %bitcast.refs_0_, ...), custom_call_target="tpu_custom_call" | custom-call | flops 5000000000 | bytes 8388608 | tf_op jit(solution)/shard_map/pallas_call | solution.py:504
  57.6 1.1 collective-permute-start.7
  58.7 8.3 %shard_map.192 = (bf16[4,4,128,512]{3,2,1,0:T(8,128)(2,1)}, bf16[4,4,128,512]{3,2,1,0:T(8,128)(2,1)}, bf16[4,4,80,512]{3,2,1,0:T(8,128)(2,1)}, bf16[4,256,512]{2,1,0:T(8,128)(2,1)}, f32[4,8,512]{2,1,0:T(8,128)}) custom-call(s32[4,6]{1,0:T(4,128)} %lengths_ref.17, s32[1]{0:T(128)} %bitcast.refs_0_, f32[2048,256]{1,0:T(8,128)} %get-tuple-element.72.refs_1_, ...), custom_call_target="tpu_custom_call" | custom-call | flops 4000000000 | bytes 8388608 | tf_op jit(solution)/shard_map/pallas_call | solution.py:504
  67.5 1.8 %collective-permute-done.8.refs_8_ = bf16[64,2304]{1,0:T(8,128)(2,1)} collective-permute-done((bf16[64,2304]{1,0:T(8,128)(2,1)}, bf16[64,2304]{1,0:T(8,128)(2,1)}, u32[]{:S(2)}, u32[]{:S(2)}) %collective-permute-start.8) | collective-permute-done | bytes 294944 | tf_op jit(solution)/shard_map/ppermute | solution.py:1017
  69.3 19.0 %shard_map.196 = (bf16[2048,256]{1,0:T(8,128)(2,1)}, f32[2048,256]{1,0:T(8,128)}, bf16[4,256,512]{2,1,0:T(8,128)(2,1)}, bf16[64,2432]{1,0:T(8,128)(2,1)}, bf16[6...) custom-call(s32[4,6]{1,0:T(4,128)} %lengths_ref.17, s32[1]{0:T(128)} %bitcast.refs_0_, ...), custom_call_target="tpu_custom_call" | custom-call | flops 10000000000 | bytes 8388608 | tf_op jit(solution)/shard_map/pallas_call | solution.py:504
  88.4 1.0 collective-permute-start.10
  90.2 21.7 %shard_map.197 = (f32[2048,256]{1,0:T(8,128)}, bf16[4,256,512]{2,1,0:T(8,128)(2,1)}, bf16[64,3200]{1,0:T(8,128)(2,1)}, bf16[64,3200]{1,0:T(8,128)(2,1)}, bf16[64...) custom-call(s32[4,6]{1,0:T(4,128)} %lengths_ref.17, s32[1]{0:T(128)} %bitcast.refs_0_, ...), custom_call_target="tpu_custom_call" | custom-call | flops 15000000512 | bytes 8388608 | tf_op jit(solution)/shard_map/pallas_call | solution.py:504
  113.8 2.1 %shard_map.198 = (bf16[32,2432]{1,0:T(8,128)(2,1)}, bf16[32,2432]{1,0:T(8,128)(2,1)}) custom-call(s32[1]{0:T(128)} %bitcast.5.place_ref, bf16[64,2432]{1,0:T(8,128)(2,1)} %get-tuple-element.77.refs_21_.refs_0_, bf16[64,2432]{1,0:T(8,128)(2,1)} %collective-permute-done.9.refs_1_, bf16[64,2432]{1,0:T(8,128)(2,1)} %collective-permute-done.10.refs_2_, ...), custom_call_target="tpu_custom_call" | custom-call | tf_op jit(solution)/shard_map/pallas_call | solution.py:921
  115.9 2.0 %collective-permute-start.12 = (bf16[32,2432]{1,0:T(8,128)(2,1)}, bf16[32,2432]{1,0:T(8,128)(2,1)}, u32[]{:S(2)}, u32[]{:S(2)}) collective-permute-start(bf16[32,2432]{1,0:T(8,128)(2,1)} %get-tuple-element.95), channel_id=1, source_target_pairs={{0,4},{4,0},{8,12},{12,8},{16,20},{20,16},{24,28},{28,24},{1,5},{5... | collective-permute-start | bytes 466952 | tf_op jit(solution)/shard_map/ppermute | solution.py:1017
  118.0 10.5 %shard_map.199 = (bf16[4,768,512]{2,1,0:T(8,128)(2,1)}, bf16[64,896]{1,0:T(8,128)(2,1)}, bf16[64,896]{1,0:T(8,128)(2,1)}, bf16[64,896]{1,0:T(8,128)(2,1)}, bf16[64,896]{1,0:T(8,128)(2,1)}) custom-call(s32[4,6]{1,0:T(4,128)} %lengths_ref.17, s32[1]{0:T(128)} %bitcast.refs_0_, bf16[2048,256]{1,0:T(8,128)(2,1)} %get-tuple-element.68.refs_1_, ...), custom_call_target="tpu_custom_call" | custom-call | flops 8000000000 | bytes 8388608 | tf_op jit(solution)/shard_map/pallas_call | solution.py:504
  130.4 1.9 %collective-permute-done.15.refs_3_ = bf16[64,3200]{1,0:T(8,128)(2,1)} collective-permute-done((bf16[64,3200]{1,0:T(8,128)(2,1)}, bf16[64,3200]{1,0:T(8,128)(2,1)}, u32[]{:S(2)}, u32[]{:S(2)}) %collective-permute-start.15) | collective-permute-done | bytes 409632 | tf_op jit(solution)/shard_map/ppermute | solution.py:1017
  132.3 2.4 %shard_map.200 = (bf16[32,3200]{1,0:T(8,128)(2,1)}, bf16[32,3200]{1,0:T(8,128)(2,1)}) custom-call(s32[1]{0:T(128)} %bitcast.5.place_ref, bf16[64,3200]{1,0:T(8,128)(2,1)} %get-tuple-element.93.refs_4_.refs_8_.refs_0_, bf16[64,3200]{1,0:T(8,128)(2,1)} %collective-permute-done.13.refs_1_, bf16[64,3200]{1,0:T(8,128)(2,1)} %collective-permute-done.14.refs_2_, ...), custom_call_target="tpu_custom_call" | custom-call | tf_op jit(solution)/shard_map/pallas_call | solution.py:921
  134.6 1.8 %collective-permute-start.16 = (bf16[32,3200]{1,0:T(8,128)(2,1)}, bf16[32,3200]{1,0:T(8,128)(2,1)}, u32[]{:S(2)}, u32[]{:S(2)}) collective-permute-start(bf16[32,3200]{1,0:T(8,128)(2,1)} %get-tuple-element.106), channel_id=1, source_target_pairs={{0,4},{4,0},{8,12},{12,8},{16,20},{20,16},{24,28},{28,24},{1,5},{5... | collective-permute-start | bytes 614408 | tf_op jit(solution)/shard_map/ppermute | solution.py:1017
  136.9 1.8 %shard_map.201 = (bf16[32,896]{1,0:T(8,128)(2,1)}, bf16[32,896]{1,0:T(8,128)(2,1)}) custom-call(s32[1]{0:T(128)} %bitcast.5.place_ref, bf16[64,896]{1,0:T(8,128)(2,1)} %get-tuple-element.107.refs_0_, bf16[64,896]{1,0:T(8,128)(2,1)} %collective-permute-done.17.refs_1_, bf16[64,896]{1,0:T(8,128)(2,1)} %collective-permute-done.18.refs_2_, ...), custom_call_target="tpu_custom_call" | custom-call | tf_op jit(solution)/shard_map/pallas_call | solution.py:921
  138.7 2.0 %collective-permute-start.20 = (bf16[32,896]{1,0:T(8,128)(2,1)}, bf16[32,896]{1,0:T(8,128)(2,1)}, u32[]{:S(2)}, u32[]{:S(2)}) collective-permute-start(bf16[32,896]{1,0:T(8,128)(2,1)} %get-tuple-element.112), channel_id=1, source_target_pairs={{0,4},{4,0},{8,12},{12,8},{16,20},{20,16},{24,28},{28,24},{1,5},{5... | collective-permute-start | bytes 172040 | tf_op jit(solution)/shard_map/ppermute | solution.py:1017
  140.7 5.4 %shard_map.202.refs_6_ = bf16[2048,256]{1,0:T(8,128)(2,1)} custom-call(s32[4,6]{1,0:T(4,128)} %lengths_ref.17, bf16[4,768,512]{2,1,0:T(8,128)(2,1)} %get-tuple-element.104.refs_5_.refs_0_, f32[2048,256]{1,0:T(8,128)} %get-tuple-element.113.refs_1_, bf16[4,64,896]{2,1,0:T(8,128)(2,1)} %get-tuple-element.71.refs_3_.refs_2_.refs_4_.refs_16_, ...), custom_call_target="tpu_custom_call" | custom-call | flops 1000000000 | bytes 6291456 | tf_op jit(solution)/shard_map/pallas_call | solution.py:504
  146.2 2.0 %shard_map.203 = (bf16[8,6528]{1,0:T(8,128)(2,1)}, bf16[8,6528]{1,0:T(8,128)(2,1)}, bf16[8,6528]{1,0:T(8,128)(2,1)}, bf16[8,6528]{1,0:T(8,128)(2,1)}) custom-call(s32[1]{0:T(128)} %bitcast.5.place_ref, bf16[32,2432]{1,0:T(8,128)(2,1)} %get-tuple-element.94.refs_9_.refs_0_, bf16[32,2432]{1,0:T(8,128)(2,1)} %collective-permute-done.12.refs_4_.refs_1_, ...), custom_call_target="tpu_custom_call" | custom-call | tf_op jit(solution)/shard_map/pallas_call | solution.py:950
  148.2 1.5 collective-permute-start.21
  149.7 2.4 %collective-permute-start.22 = (bf16[8,6528]{1,0:T(8,128)(2,1)}, bf16[8,6528]{1,0:T(8,128)(2,1)}, u32[]{:S(2)}, u32[]{:S(2)}) collective-permute-start(bf16[8,6528]{1,0:T(8,128)(2,1)} %get-tuple-element.116), channel_id=1, source_target_pairs={{0,16},{4,20},{8,24},{12,28},{16,0},{20,4},{24,8},{28,12},{1,17},{... | collective-permute-start | bytes 313352 | tf_op jit(solution)/shard_map/ppermute | solution.py:1017
  152.6 3.9 %shard_map.204.refs_4_ = bf16[2048,256]{1,0:T(8,128)(2,1)} custom-call(s32[4,6]{1,0:T(4,128)} %lengths_ref.17, bf16[2048,256]{1,0:T(8,128)(2,1)} %get-tuple-element.76.refs_0_, bf16[8,6528]{1,0:T(8,128)(2,1)} %get-tuple-element.114.refs_1_.refs_0_), custom_call_target="tpu_custom_call" | custom-call | flops 3000000000 | bytes 8388608 | tf_op jit(solution)/shard_map/pallas_call | solution.py:504
  156.5 4.7 %collective-permute-done.22.refs_2_ = bf16[8,6528]{1,0:T(8,128)(2,1)} collective-permute-done((bf16[8,6528]{1,0:T(8,128)(2,1)}, bf16[8,6528]{1,0:T(8,128)(2,1)}, u32[]{:S(2)}, u32[]{:S(2)}) %collective-permute-start.22) | collective-permute-done | bytes 104480 | tf_op jit(solution)/shard_map/ppermute | solution.py:1017
  161.2 1.7 %shard_map.205 = (f32[2,8,768]{2,1,0:T(8,128)}, f32[2,2,8]{2,1,0:T(2,128)}, f32[2,8,256]{2,1,0:T(8,128)}, f32[2,8,1024]{2,1,0:T(8,128)}, f32[2,32]{1,0:T(2,128)}...) custom-call(bf16[8,6528]{1,0:T(8,128)(2,1)} %get-tuple-element.114.refs_1_.refs_0_, ...), custom_call_target="tpu_custom_call" | custom-call | tf_op jit(solution)/shard_map/pallas_call | solution.py:1002
  (50 shorter events, 9.3 us)
Async XLA Ops:
  2.4 21.5 %all-to-all-start = ((bf16[8,8,3968]{2,1,0:T(8,128)(2,1)}), bf16[8,8,3968]{2,1,0:T(8,128)(2,1)}, u32[]{:S(2)}, u32[]{:S(2)}) async-start(bf16[8,8,3968]{2,1,0:T(8,128)(2,1)} %bitcast.7), calls=%async_computation | async-start | bytes 1015808 | tf_op jit(solution)/shard_map/all_to_all | solution.py:1012
  24.8 1.7 %copy-start = (bf16[64,896]{1,0:T(8,128)(2,1)}, bf16[64,896]{1,0:T(8,128)(2,1)S(1)}, u32[]{:S(2)}) copy-start(bf16[64,896]{1,0:T(8,128)(2,1)S(1)} %slice.8.refs_2_) | copy-start | bytes 344068
  24.8 5.4 %collective-permute-start.2 = (bf16[64,896]{1,0:T(8,128)(2,1)S(1)}, bf16[64,896]{1,0:T(8,128)(2,1)S(1)}, u32[]{:S(2)}, u32[]{:S(2)}) collective-permute-start(bf16[64,896]{1,0:T(8,128)(2,1)S(1)} %slice.8.refs_2_), channel_id=1, source_target_pairs={{0,3},{1,2},{2,1},{3,0},{4,7},{5,6},{6,5},{7,4},{8,11},{9,10},{10,... | collective-permute-start | bytes 344072 | tf_op jit(solution)/shard_map/ppermute | solution.py:1017
  24.9 8.0 %collective-permute-start.1 = (bf16[64,896]{1,0:T(8,128)(2,1)S(1)}, bf16[64,896]{1,0:T(8,128)(2,1)S(1)}, u32[]{:S(2)}, u32[]{:S(2)}) collective-permute-start(bf16[64,896]{1,0:T(8,128)(2,1)S(1)} %slice.8.refs_2_), channel_id=1, source_target_pairs={{0,2},{1,3},{2,0},{3,1},{4,6},{5,7},{6,4},{7,5},{8,10},{9,11},{10,... | collective-permute-start | bytes 344072 | tf_op jit(solution)/shard_map/ppermute | solution.py:1017
  26.5 6.4 %collective-permute-start = (bf16[64,896]{1,0:T(8,128)(2,1)S(1)}, bf16[64,896]{1,0:T(8,128)(2,1)S(1)}, u32[]{:S(2)}, u32[]{:S(2)}) collective-permute-start(bf16[64,896]{1,0:T(8,128)(2,1)S(1)} %slice.8.refs_2_), channel_id=1, source_target_pairs={{0,1},{1,0},{2,3},{3,2},{4,5},{5,4},{6,7},{7,6},{8,9},{9,8},{10,11... | collective-permute-start | bytes 344072 | tf_op jit(solution)/shard_map/ppermute | solution.py:1017
  28.5 13.2 %collective-permute-start.4 = (bf16[64,3072]{1,0:T(8,128)(2,1)}, bf16[64,3072]{1,0:T(8,128)(2,1)}, u32[]{:S(2)}, u32[]{:S(2)}) collective-permute-start(bf16[64,3072]{1,0:T(8,128)(2,1)} %slice.9.refs_4_.refs_3_.refs_17_), channel_id=1, source_target_pairs={{0,2},{1,3},{2,0},{3,1},{4,6},{5,7},{6,4},{7,5},{8,10},{9,11},{10,... | collective-permute-start | bytes 1179656 | tf_op jit(solution)/shard_map/ppermute | solution.py:1017
  30.1 16.1 %collective-permute-start.3 = (bf16[64,3072]{1,0:T(8,128)(2,1)}, bf16[64,3072]{1,0:T(8,128)(2,1)}, u32[]{:S(2)}, u32[]{:S(2)}) collective-permute-start(bf16[64,3072]{1,0:T(8,128)(2,1)} %slice.9.refs_4_.refs_3_.refs_17_), channel_id=1, source_target_pairs={{0,1},{1,0},{2,3},{3,2},{4,5},{5,4},{6,7},{7,6},{8,9},{9,8},{10,11... | collective-permute-start | bytes 1179656 | tf_op jit(solution)/shard_map/ppermute | solution.py:1017
  30.3 2.6 %copy-start.1 = (bf16[64,896]{1,0:T(8,128)(2,1)}, bf16[64,896]{1,0:T(8,128)(2,1)S(1)}, u32[]{:S(2)}) copy-start(bf16[64,896]{1,0:T(8,128)(2,1)S(1)} %collective-permute-done.2.refs_5_) | copy-start | bytes 344068
  32.9 0.6 copy-start.2
  33.5 0.6 copy-start.3
  41.8 4.4 %collective-permute-start.5 = (bf16[64,3072]{1,0:T(8,128)(2,1)}, bf16[64,3072]{1,0:T(8,128)(2,1)}, u32[]{:S(2)}, u32[]{:S(2)}) collective-permute-start(bf16[64,3072]{1,0:T(8,128)(2,1)} %shard_map.190.refs_6_.refs_5_.refs_19_), channel_id=1, source_target_pairs={{0,1},{1,0},{2,3},{3,2},{4,5},{5,4},{6,7},{7,6},{8,9},{9,8},{10,11... | collective-permute-start | bytes 1179656 | tf_op jit(solution)/shard_map/ppermute | solution.py:1017
  41.9 15.7 %all-to-all-start.1 = ((bf16[8,8,2304]{2,1,0:T(8,128)(2,1)}), bf16[8,8,2304]{2,1,0:T(8,128)(2,1)}, u32[]{:S(2)}, u32[]{:S(2)}) async-start(bf16[8,8,2304]{2,1,0:T(8,128)(2,1)} %bitcast.6), calls=%async_computation.1 | async-start | bytes 589824 | tf_op jit(solution)/shard_map/all_to_all | solution.py:1012
  57.6 9.8 %collective-permute-start.7 = (bf16[64,2304]{1,0:T(8,128)(2,1)}, bf16[64,2304]{1,0:T(8,128)(2,1)}, u32[]{:S(2)}, u32[]{:S(2)}) collective-permute-start(bf16[64,2304]{1,0:T(8,128)(2,1)} %shard_map.194.refs_5_), channel_id=1, source_target_pairs={{0,2},{1,3},{2,0},{3,1},{4,6},{5,7},{6,4},{7,5},{8,10},{9,11},{10,... | collective-permute-start | bytes 884744 | tf_op jit(solution)/shard_map/ppermute | solution.py:1017
  58.7 8.8 %collective-permute-start.6 = (bf16[64,2304]{1,0:T(8,128)(2,1)}, bf16[64,2304]{1,0:T(8,128)(2,1)}, u32[]{:S(2)}, u32[]{:S(2)}) collective-permute-start(bf16[64,2304]{1,0:T(8,128)(2,1)} %shard_map.194.refs_5_), channel_id=1, source_target_pairs={{0,1},{1,0},{2,3},{3,2},{4,5},{5,4},{6,7},{7,6},{8,9},{9,8},{10,11... | collective-permute-start | bytes 884744 | tf_op jit(solution)/shard_map/ppermute | solution.py:1017
  67.3 1.9 %collective-permute-start.8 = (bf16[64,2304]{1,0:T(8,128)(2,1)}, bf16[64,2304]{1,0:T(8,128)(2,1)}, u32[]{:S(2)}, u32[]{:S(2)}) collective-permute-start(bf16[64,2304]{1,0:T(8,128)(2,1)} %shard_map.195.refs_7_), channel_id=1, source_target_pairs={{0,1},{1,0},{2,3},{3,2},{4,5},{5,4},{6,7},{7,6},{8,9},{9,8},{10,11... | collective-permute-start | bytes 884744 | tf_op jit(solution)/shard_map/ppermute | solution.py:1017
  88.2 25.1 %collective-permute-start.9 = (bf16[64,2432]{1,0:T(8,128)(2,1)}, bf16[64,2432]{1,0:T(8,128)(2,1)}, u32[]{:S(2)}, u32[]{:S(2)}) collective-permute-start(bf16[64,2432]{1,0:T(8,128)(2,1)} %get-tuple-element.78), channel_id=1, source_target_pairs={{0,1},{1,0},{2,3},{3,2},{4,5},{5,4},{6,7},{7,6},{8,9},{9,8},{10,11... | collective-permute-start | bytes 933896 | tf_op jit(solution)/shard_map/ppermute | solution.py:1017
  88.4 25.3 %collective-permute-start.10 = (bf16[64,2432]{1,0:T(8,128)(2,1)}, bf16[64,2432]{1,0:T(8,128)(2,1)}, u32[]{:S(2)}, u32[]{:S(2)}) collective-permute-start(bf16[64,2432]{1,0:T(8,128)(2,1)} %get-tuple-element.79), channel_id=1, source_target_pairs={{0,2},{1,3},{2,0},{3,1},{4,6},{5,7},{6,4},{7,5},{8,10},{9,11},{10,... | collective-permute-start | bytes 933896 | tf_op jit(solution)/shard_map/ppermute | solution.py:1017
  89.4 24.3 %collective-permute-start.11 = (bf16[64,2432]{1,0:T(8,128)(2,1)}, bf16[64,2432]{1,0:T(8,128)(2,1)}, u32[]{:S(2)}, u32[]{:S(2)}) collective-permute-start(bf16[64,2432]{1,0:T(8,128)(2,1)} %get-tuple-element.80), channel_id=1, source_target_pairs={{0,3},{1,2},{2,1},{3,0},{4,7},{5,6},{6,5},{7,4},{8,11},{9,10},{10,... | collective-permute-start | bytes 933896 | tf_op jit(solution)/shard_map/ppermute | solution.py:1017
  111.9 17.1 %collective-permute-start.13 = (bf16[64,3200]{1,0:T(8,128)(2,1)}, bf16[64,3200]{1,0:T(8,128)(2,1)}, u32[]{:S(2)}, u32[]{:S(2)}) collective-permute-start(bf16[64,3200]{1,0:T(8,128)(2,1)} %get-tuple-element.96), channel_id=1, source_target_pairs={{0,1},{1,0},{2,3},{3,2},{4,5},{5,4},{6,7},{7,6},{8,9},{9,8},{10,11... | collective-permute-start | bytes 1228808 | tf_op jit(solution)/shard_map/ppermute | solution.py:1017
  112.3 17.3 %collective-permute-start.14 = (bf16[64,3200]{1,0:T(8,128)(2,1)}, bf16[64,3200]{1,0:T(8,128)(2,1)}, u32[]{:S(2)}, u32[]{:S(2)}) collective-permute-start(bf16[64,3200]{1,0:T(8,128)(2,1)} %get-tuple-element.97), channel_id=1, source_target_pairs={{0,2},{1,3},{2,0},{3,1},{4,6},{5,7},{6,4},{7,5},{8,10},{9,11},{10,... | collective-permute-start | bytes 1228808 | tf_op jit(solution)/shard_map/ppermute | solution.py:1017
  113.3 18.9 %collective-permute-start.15 = (bf16[64,3200]{1,0:T(8,128)(2,1)}, bf16[64,3200]{1,0:T(8,128)(2,1)}, u32[]{:S(2)}, u32[]{:S(2)}) collective-permute-start(bf16[64,3200]{1,0:T(8,128)(2,1)} %get-tuple-element.98), channel_id=1, source_target_pairs={{0,3},{1,2},{2,1},{3,0},{4,7},{5,6},{6,5},{7,4},{8,11},{9,10},{10,... | collective-permute-start | bytes 1228808 | tf_op jit(solution)/shard_map/ppermute | solution.py:1017
  115.9 16.3 %collective-permute-start.12 = (bf16[32,2432]{1,0:T(8,128)(2,1)}, bf16[32,2432]{1,0:T(8,128)(2,1)}, u32[]{:S(2)}, u32[]{:S(2)}) collective-permute-start(bf16[32,2432]{1,0:T(8,128)(2,1)} %get-tuple-element.95), channel_id=1, source_target_pairs={{0,4},{4,0},{8,12},{12,8},{16,20},{20,16},{24,28},{28,24},{1,5},{5... | collective-permute-start | bytes 466952 | tf_op jit(solution)/shard_map/ppermute | solution.py:1017
  128.4 8.0 %collective-permute-start.17 = (bf16[64,896]{1,0:T(8,128)(2,1)}, bf16[64,896]{1,0:T(8,128)(2,1)}, u32[]{:S(2)}, u32[]{:S(2)}) collective-permute-start(bf16[64,896]{1,0:T(8,128)(2,1)} %get-tuple-element.108), channel_id=1, source_target_pairs={{0,1},{1,0},{2,3},{3,2},{4,5},{5,4},{6,7},{7,6},{8,9},{9,8},{10,11... | collective-permute-start | bytes 344072 | tf_op jit(solution)/shard_map/ppermute | solution.py:1017
  128.9 7.5 %collective-permute-start.18 = (bf16[64,896]{1,0:T(8,128)(2,1)}, bf16[64,896]{1,0:T(8,128)(2,1)}, u32[]{:S(2)}, u32[]{:S(2)}) collective-permute-start(bf16[64,896]{1,0:T(8,128)(2,1)} %get-tuple-element.109), channel_id=1, source_target_pairs={{0,2},{1,3},{2,0},{3,1},{4,6},{5,7},{6,4},{7,5},{8,10},{9,11},{10,... | collective-permute-start | bytes 344072 | tf_op jit(solution)/shard_map/ppermute | solution.py:1017
  129.6 7.3 %collective-permute-start.19 = (bf16[64,896]{1,0:T(8,128)(2,1)}, bf16[64,896]{1,0:T(8,128)(2,1)}, u32[]{:S(2)}, u32[]{:S(2)}) collective-permute-start(bf16[64,896]{1,0:T(8,128)(2,1)} %get-tuple-element.110), channel_id=1, source_target_pairs={{0,3},{1,2},{2,1},{3,0},{4,7},{5,6},{6,5},{7,4},{8,11},{9,10},{10,... | collective-permute-start | bytes 344072 | tf_op jit(solution)/shard_map/ppermute | solution.py:1017
  134.6 11.5 %collective-permute-start.16 = (bf16[32,3200]{1,0:T(8,128)(2,1)}, bf16[32,3200]{1,0:T(8,128)(2,1)}, u32[]{:S(2)}, u32[]{:S(2)}) collective-permute-start(bf16[32,3200]{1,0:T(8,128)(2,1)} %get-tuple-element.106), channel_id=1, source_target_pairs={{0,4},{4,0},{8,12},{12,8},{16,20},{20,16},{24,28},{28,24},{1,5},{5... | collective-permute-start | bytes 614408 | tf_op jit(solution)/shard_map/ppermute | solution.py:1017
  138.7 7.4 %collective-permute-start.20 = (bf16[32,896]{1,0:T(8,128)(2,1)}, bf16[32,896]{1,0:T(8,128)(2,1)}, u32[]{:S(2)}, u32[]{:S(2)}) collective-permute-start(bf16[32,896]{1,0:T(8,128)(2,1)} %get-tuple-element.112), channel_id=1, source_target_pairs={{0,4},{4,0},{8,12},{12,8},{16,20},{20,16},{24,28},{28,24},{1,5},{5... | collective-permute-start | bytes 172040 | tf_op jit(solution)/shard_map/ppermute | solution.py:1017
  148.2 8.3 %collective-permute-start.21 = (bf16[8,6528]{1,0:T(8,128)(2,1)}, bf16[8,6528]{1,0:T(8,128)(2,1)}, u32[]{:S(2)}, u32[]{:S(2)}) collective-permute-start(bf16[8,6528]{1,0:T(8,128)(2,1)} %get-tuple-element.115), channel_id=1, source_target_pairs={{0,8},{4,12},{8,0},{12,4},{16,24},{20,28},{24,16},{28,20},{1,9},{5... | collective-permute-start | bytes 313352 | tf_op jit(solution)/shard_map/ppermute | solution.py:1017
  149.7 11.5 %collective-permute-start.22 = (bf16[8,6528]{1,0:T(8,128)(2,1)}, bf16[8,6528]{1,0:T(8,128)(2,1)}, u32[]{:S(2)}, u32[]{:S(2)}) collective-permute-start(bf16[8,6528]{1,0:T(8,128)(2,1)} %get-tuple-element.116), channel_id=1, source_target_pairs={{0,16},{4,20},{8,24},{12,28},{16,0},{20,4},{24,8},{28,12},{1,17},{... | collective-permute-start | bytes 313352 | tf_op jit(solution)/shard_map/ppermute | solution.py:1017
  152.0 9.1 %collective-permute-start.23 = (bf16[8,6528]{1,0:T(8,128)(2,1)}, bf16[8,6528]{1,0:T(8,128)(2,1)}, u32[]{:S(2)}, u32[]{:S(2)}) collective-permute-start(bf16[8,6528]{1,0:T(8,128)(2,1)} %get-tuple-element.117), channel_id=1, source_target_pairs={{0,24},{4,28},{8,16},{12,20},{16,8},{20,12},{24,0},{28,4},{1,25},{... | collective-permute-start | bytes 313352 | tf_op jit(solution)/shard_map/ppermute | solution.py:1017
